TPU v7x, 32 devices: a whole 2x2x4 slice. The times are simulated.
32 devices in a mesh: gx: 4 (over y, x), gy: 8 (over z, core).
Axes of the slice: x: 2, y: 2, z: 4, core: 2. Of those that a mesh axis runs over, the one named last changes fastest.
Arguments:
- gas_pos: float32 [512, 3, 128], P(('gx', 'gy')), may hold values from -6 to 6
- gas_vel: float32 [512, 3, 128], P(('gx', 'gy')), may hold values from -4 to 4
- gas_mass: float32 [512, 128], P(('gx', 'gy')), may hold values from 0.5 to 2
- gas_smooth: float32 [512, 128], P(('gx', 'gy')), may hold values from 0.3 to 1
- gas_energy: float32 [512, 128], P(('gx', 'gy')), may hold values from 1 to 3
- gas_metals: float32 [512, 16, 128], P(('gx', 'gy')), may hold values from 0.001 to 0.05
- gas_bins: int32 [512], P(('gx', 'gy')), may hold values from 0 to 2
- gas_nbr_dev: int32 [512, 8], P(('gx', 'gy')), may hold values from 0 to 31, all different within a row; in each aligned block of 16 rows (0 to 15, 16 to 31, ...) at most 8 rows name the same one
- gas_nbr_slot: int32 [512, 8], P(('gx', 'gy')), may hold values from 0 to 15
- star_pos: float32 [256, 3, 128], P(('gx', 'gy')), may hold values from -2.5 to 2.5
- star_vel: float32 [256, 3, 128], P(('gx', 'gy')), may hold values from -3 to 3
- star_radius: float32 [256, 128], P(('gx', 'gy')), may hold values from 0.5 to 1.5
- star_mdot: float32 [256, 128], P(('gx', 'gy')), may hold values from 3 to 24
- star_edot: float32 [256, 128], P(('gx', 'gy')), may hold values from 1 to 8
- star_yields: float32 [256, 16, 128], P(('gx', 'gy')), may hold values from 0.02 to 0.2
- star_ovl_dev: int32 [256, 16], P(('gx', 'gy')), may hold values from 0 to 31, all different within a row; in each aligned block of 8 rows (0 to 7, 8 to 15, ...) at most 8 rows name the same one
- star_ovl_slot: int32 [256, 16], P(('gx', 'gy')), may hold values from 0 to 15
Outputs:
- final_pos: float32 [512, 3, 128], P(('gx', 'gy'))
- final_vel: float32 [512, 3, 128], P(('gx', 'gy'))
- final_mass: float32 [512, 128], P(('gx', 'gy'))
- final_energy: float32 [512, 128], P(('gx', 'gy'))
- final_metals: float32 [512, 16, 128], P(('gx', 'gy'))
Inputs may be any that keep to these rules, and one draw needn't show every extreme that they name: `gas_nbr_dev`: each gas block names 8 different devices; among the gas blocks of one device no device is named more than 8 times, and some device exactly 8 times. `star_ovl_dev`: each star block names 16 different devices; among the star blocks of one device no device is named more than 8 times, and some device exactly 8 times.
All inputs are finite; a program needn't handle non-finite values.
Results may differ from a plain program's by a relative error of at most 0.00011.
Values sent between devices are 32-bit elements; how exact they have to be, the bound alone decides.
No kernel may reach another device: no remote copies, remote signals or barrier semaphores. Data moves between devices by JAX's collectives and lax.ppermute only.
A program may use at most 64 MiB of HBM per device.

v0:
```python
import jax
import jax.numpy as jnp
from jax import lax
from jax.sharding import PartitionSpec as P

SUBSTEPS = 4


KERNEL_NORM = 0.1795871221251666
GAMMA_LESS = 0.6666666666666666
TIME_STEP = 0.05
COOL_RATE = 0.4
ENERGY_FLOOR = 0.2


def kernel(dist_sq, smooth):
    return KERNEL_NORM * jnp.exp(-dist_sq / (smooth * smooth)) / (smooth * smooth * smooth)


def geometry(own_pos, far_pos):
    offset = own_pos[None, :, :, None] - far_pos[:, :, None, :]
    return (offset, jnp.sum(offset * offset, axis=1))


def block_density(own_pos, own_smooth, far_pos, far_mass):
    offset, dist_sq = geometry(own_pos, far_pos)
    weight = kernel(dist_sq, own_smooth[None, :, None])
    return jnp.sum(far_mass[:, None, :] * weight, axis=(0, 2))


def block_force(
    own_pos, own_vel, own_smooth, own_term, far_pos, far_vel, far_mass, far_smooth, far_term
):
    offset, dist_sq = geometry(own_pos, far_pos)
    own_width = own_smooth[None, :, None]
    far_width = far_smooth[:, None, :]
    own_grad = 2.0 * kernel(dist_sq, own_width) / (own_width * own_width)
    far_grad = 2.0 * kernel(dist_sq, far_width) / (far_width * far_width)
    coupling = far_mass[:, None, :] * (
        own_term[None, :, None] * own_grad + far_term[:, None, :] * far_grad
    )
    acceleration = jnp.sum(coupling[:, None] * offset, axis=(0, 3))
    velocity_gap = own_vel[None, :, :, None] - far_vel[:, :, None, :]
    converge = jnp.sum(velocity_gap * offset, axis=1)
    heating = -own_term * jnp.sum(far_mass[:, None, :] * own_grad * converge, axis=(0, 2))
    return (acceleration, heating)


def star_deposit(star_now, star_reach, star_rate, star_power, star_speed, star_yield, gas_near):
    gas_place = gas_near[:, 0:3]
    gas_width = gas_near[:, 3]
    offset = star_now[None, :, :, None] - gas_place[:, :, None, :]
    dist_sq = jnp.sum(offset * offset, axis=1)
    width_sq = gas_width[:, None, :] * gas_width[:, None, :]
    solid = 0.5 * (1.0 - jnp.sqrt(dist_sq) / jnp.sqrt(dist_sq + width_sq))
    omega = solid * jnp.exp(-dist_sq / (star_reach[None, :, None] * star_reach[None, :, None]))
    total = jnp.sum(omega, axis=(0, 2))
    share = omega / total[None, :, None]
    ejecta = star_rate * TIME_STEP
    payload = jnp.concatenate(
        [
            ejecta[None],
            ejecta[None] * star_speed,
            (star_power * TIME_STEP)[None],
            ejecta[None] * star_yield,
        ],
        axis=0,
    )
    return jnp.einsum("qs,lsg->lqg", payload, share, precision=lax.Precision.HIGHEST)


def absorb(gas_mass_now, gas_vel_now, gas_heat, gas_metal, deposit):
    new_mass = gas_mass_now + deposit[:, 0]
    new_vel = (gas_mass_now[:, None] * gas_vel_now + deposit[:, 1:4]) / new_mass[:, None]
    new_energy = (gas_mass_now * gas_heat + deposit[:, 4]) / new_mass
    new_metal = gas_metal + deposit[:, 5:]
    return (new_mass, new_vel, new_energy, new_metal)


def cooling(energy_now, density):
    return ENERGY_FLOOR + (energy_now - ENERGY_FLOOR) * jnp.exp(-TIME_STEP * COOL_RATE * density)


def density_of(inputs):
    own_block, beside_all = inputs
    return block_density(own_block[0:3], own_block[7], beside_all[:, 0:3], beside_all[:, 6])


def force_of(own_block, beside_all, term_own, term_near):
    return block_force(
        own_block[0:3],
        own_block[3:6],
        own_block[7],
        term_own,
        beside_all[:, 0:3],
        beside_all[:, 3:6],
        beside_all[:, 6],
        beside_all[:, 7],
        term_near,
    )


def force_dense(inputs):
    own_block, beside_all, term_own, term_near, flag = inputs
    return force_of(own_block, beside_all, term_own, term_near)


def deposit_of(inputs):
    return star_deposit(inputs[0], inputs[1], inputs[2], inputs[3], inputs[4], inputs[5], inputs[6])


def request_plan(destination, slot_ids, peer_count, capacity):
    flat_dest = destination.reshape(-1)
    flat_slot = slot_ids.reshape(-1)
    matches = (flat_dest[:, None] == jnp.arange(peer_count, dtype=jnp.int32)[None, :]).astype(
        jnp.int32
    )
    earlier = jnp.cumsum(matches, axis=0) - matches
    queue_place = jnp.sum(earlier * matches, axis=1)
    places = flat_dest * capacity + queue_place
    wanted = jnp.full((peer_count * capacity,), -1, jnp.int32).at[places].set(flat_slot)
    return (places, wanted.reshape(peer_count, capacity))


def trade_requests(gas_wanted, star_wanted):
    return (
        lax.all_to_all(gas_wanted, ("gx", "gy"), split_axis=0, concat_axis=0, tiled=True),
        lax.all_to_all(star_wanted, ("gx", "gy"), split_axis=0, concat_axis=0, tiled=True),
    )


def trade_ghosts(payload):
    return lax.all_to_all(payload, ("gx", "gy"), split_axis=0, concat_axis=0, tiled=True)


def trade_terms(payload):
    return lax.all_to_all(payload, ("gx", "gy"), split_axis=0, concat_axis=0, tiled=True)


def trade_places(payload):
    return lax.all_to_all(payload, ("gx", "gy"), split_axis=0, concat_axis=0, tiled=True)


def trade_deposits(payload):
    return lax.all_to_all(payload, ("gx", "gy"), split_axis=0, concat_axis=0, tiled=True)


def local(
    gas_pos,
    gas_vel,
    gas_mass,
    gas_smooth,
    gas_energy,
    gas_metals,
    gas_bins,
    gas_nbr_dev,
    gas_nbr_slot,
    star_pos,
    star_vel,
    star_radius,
    star_mdot,
    star_edot,
    star_yields,
    star_ovl_dev,
    star_ovl_slot,
):
    peer_count = lax.axis_size(("gx", "gy"))
    local_blocks = gas_pos.shape[0]
    neighbours = gas_nbr_dev.shape[1]
    star_blocks = star_pos.shape[0]
    intersections = star_ovl_dev.shape[1]
    width = gas_pos.shape[2]
    gas_cap = max(2, 2 * local_blocks * neighbours // peer_count)
    star_cap = max(2, 2 * star_blocks * intersections // peer_count)
    entries = peer_count * star_cap
    gas_places, gas_wanted = request_plan(gas_nbr_dev, gas_nbr_slot, peer_count, gas_cap)
    star_places, star_wanted = request_plan(star_ovl_dev, star_ovl_slot, peer_count, star_cap)
    gas_asked, star_asked = trade_requests(gas_wanted, star_wanted)
    gas_pick = jnp.maximum(gas_asked, 0)
    star_pick = jnp.maximum(star_asked, 0)
    star_owner = (
        star_asked.reshape(-1)[:, None] == jnp.arange(local_blocks, dtype=jnp.int32)[None, :]
    ).astype(jnp.float32)
    period = jnp.where(gas_bins == 0, 1, jnp.where(gas_bins == 1, 2, 4)).astype(jnp.int32)
    position, velocity, masses, energy, metals = (
        gas_pos,
        gas_vel,
        gas_mass,
        gas_energy,
        gas_metals,
    )
    for substep in range(SUBSTEPS):
        gas_state = jnp.concatenate(
            [position, velocity, masses[:, None], gas_smooth[:, None], energy[:, None]], axis=1
        )
        arrived = trade_ghosts(gas_state[gas_pick])
        ghosts = arrived.reshape((peer_count * gas_cap,) + arrived.shape[2:])[gas_places]
        ghosts = ghosts.reshape((local_blocks, neighbours) + arrived.shape[2:])
        near_state = jnp.concatenate([gas_state[:, None], ghosts], axis=1)
        density = lax.map(density_of, (gas_state, near_state))
        own_term = GAMMA_LESS * energy / density
        far_terms = trade_terms(own_term[gas_pick])
        far_terms = far_terms.reshape(peer_count * gas_cap, width)[gas_places].reshape(
            local_blocks, neighbours, width
        )
        near_term = jnp.concatenate([own_term[:, None], far_terms], axis=1)
        active = (substep % period == 0).astype(jnp.float32)
        kick_time = active * TIME_STEP * period.astype(jnp.float32)
        acceleration, heating = lax.map(
            force_dense, (gas_state, near_state, own_term, near_term, active)
        )
        velocity = velocity + kick_time[:, None, None] * acceleration
        energy = energy + kick_time[:, None] * heating
        position = position + TIME_STEP * velocity
        gas_reach = jnp.concatenate([position, gas_smooth[:, None]], axis=1)
        star_now = star_pos + (substep + 1) * TIME_STEP * star_vel
        reach_back = trade_places(gas_reach[star_pick])
        star_near = reach_back.reshape((entries,) + reach_back.shape[2:])[star_places]
        star_near = star_near.reshape((star_blocks, intersections) + reach_back.shape[2:])
        star_parts = lax.map(
            deposit_of,
            (star_now, star_radius, star_mdot, star_edot, star_vel, star_yields, star_near),
        )
        outgoing = jnp.zeros((entries,) + star_parts.shape[2:], jnp.float32)
        outgoing = outgoing.at[star_places].set(star_parts.reshape((-1,) + star_parts.shape[2:]))
        incoming = trade_deposits(outgoing.reshape((peer_count, star_cap) + star_parts.shape[2:]))
        loads = incoming.shape[-2]
        energy = cooling(energy, density)
        deposit = jnp.einsum(
            "eg,ef->gf", star_owner, incoming.reshape(entries, -1), precision=lax.Precision.HIGHEST
        )
        deposit = deposit.reshape(local_blocks, loads, width)
        masses, velocity, energy, metals = absorb(masses, velocity, energy, metals, deposit)
    return (position, velocity, masses, energy, metals)


def solution(mesh):
    placed = (
        P(("gx", "gy"), None, None),
        P(("gx", "gy"), None, None),
        P(("gx", "gy"), None),
        P(("gx", "gy"), None),
        P(("gx", "gy"), None),
        P(("gx", "gy"), None, None),
        P(("gx", "gy")),
        P(("gx", "gy"), None),
        P(("gx", "gy"), None),
        P(("gx", "gy"), None, None),
        P(("gx", "gy"), None, None),
        P(("gx", "gy"), None),
        P(("gx", "gy"), None),
        P(("gx", "gy"), None),
        P(("gx", "gy"), None, None),
        P(("gx", "gy"), None),
        P(("gx", "gy"), None),
    )
    return jax.shard_map(
        local,
        mesh=mesh,
        in_specs=placed,
        out_specs=(
            P(("gx", "gy"), None, None),
            P(("gx", "gy"), None, None),
            P(("gx", "gy"), None),
            P(("gx", "gy"), None),
            P(("gx", "gy"), None, None),
        ),
        check_vma=False,
    )
```

profile of v0, /device:TPU:1, one launch (start us, length us, event | category | flops | bytes accessed | tf_op | source)
XLA Modules:
  0.0 989.0 jit_solution(15177329009117068633)
XLA Ops:
  5.1 7.1 all-to-all-start.3
  16.9 2.0 all-to-all-done.3
  18.9 3.8 all-to-all-start
  24.2 1.5 concatenate.60
  25.7 3.7 all-to-all-done
  31.8 1.5 copy.395
  33.4 3.0 all-to-all-start.1
  37.2 29.1 %all-to-all-done.1 = f32[32,8,9,128]{3,1,2,0:T(8,128)S(1)} async-done(((f32[32,8,9,128]{3,1,2,0:T(8,128)}), f32[32,8,9,128]{3,1,2,0:T(8,128)S(1)}, u32[]{:S(2)}, u32[]{:S(2)}) %all-to-all-start.1) | async-done | bytes 1179680 | tf_op jit(solution)/shard_map/all_to_all | solution.py:133
  68.3 11.2 %while.128 = (s32[]{:T(128)}, f32[16,128]{1,0:T(8,128)S(1)}, f32[16,9,9,128]{3,1,2,0:T(8,128)S(1)}, f32[16,9,128]{2,1,0:T(8,128)S(1)}, s32[]{:T(128)}, /*index=5*/s32[]{:T(128)}, s32[]{}) while((s32[]{:T(128)}, f32[16,128]{1,0:T(8,128)S(1)}, f32[16,9,9,128]{3,1,2,0:T(8,128)S(1)}, f32[16,9,128]{2,1,0:T(8,128)S(1)}, s32[]{:T(128)}, ...), condition=%wide.region_6.7_spmd, body=%wide.region_3.0_spmd.sunk | while | flops 2064515 | bytes 1354349 | solution.py:200
  80.9 3.0 all-to-all-start.2
  84.7 7.6 all-to-all-done.2
  93.0 30.2 %while.129 = (s32[]{:T(128)}, f32[16,3,128]{2,0,1:T(8,128)S(1)}, f32[16,128]{1,0:T(8,128)S(1)}, f32[16,9,9,128]{3,1,2,0:T(8,128)S(1)}, f32[16,128]{1,0:T(8,128)S...) while((s32[]{:T(128)}, f32[16,3,128]{2,0,1:T(8,128)S(1)}, ...), condition=%wide.region_12.13_spmd, body=%wide.region_7.12_spmd.sunk | while | flops 7227652 | bytes 4445869 | solution.py:209
  123.4 1.7 gather_fusion.4
  125.2 3.1 all-to-all-start.4
  129.0 15.4 %all-to-all-done.4 = f32[32,8,4,128]{3,2,1,0:T(4,128)S(1)} async-done(((f32[32,8,4,128]{3,2,1,0:T(4,128)}), f32[32,8,4,128]{3,2,1,0:T(4,128)S(1)}, u32[]{:S(2)}, u32[]{:S(2)}) %all-to-all-start.4) | async-done | bytes 524320 | tf_op jit(solution)/shard_map/all_to_all | solution.py:141
  145.3 31.5 %while.130 = (s32[]{:T(128)}, f32[8,16,21,128]{3,2,1,0:T(8,128)S(1)}, f32[8,3,128]{2,1,0:T(4,128)S(1)}, f32[8,16,4,128]{3,2,1,0:T(4,128)S(1)}, f32[8,128]{1,0:T(...) while((s32[]{:T(128)}, ...), condition=%wide.region_19.20_spmd, body=%wide.region_16.19_spmd.sunk | while | flops 72364544 | bytes 3670657 | solution.py:220
  178.1 11.7 %scatter_fusion = f32[256,21,128]{2,1,0:T(8,128)S(1)} fusion(f32[256,21,128]{2,1,0:T(8,128)S(1)} %broadcast.472.clone, s32[128]{0:T(128)S(1)} %fusion.148, f32[128,21,128]{2,1,0:T(8,128)} %bitcast.615), kind=kCustom, calls=%fused_computation.26 | custom fusion | bytes 4129280 | tf_op jit(solution)/shard_map/scatter | solution.py:225
  189.8 2.0 copy.410
  191.9 2.9 all-to-all-start.5
  194.9 63.6 %all-to-all-done.5 = f32[32,8,21,128]{3,1,2,0:T(8,128)S(1)} async-done(((f32[32,8,21,128]{3,1,2,0:T(8,128)}), f32[32,8,21,128]{3,1,2,0:T(8,128)S(1)}, u32[]{:S(2)}, u32[]{:S(2)}) %all-to-all-start.5) | async-done | bytes 2752544 | tf_op jit(solution)/shard_map/all_to_all | solution.py:145
  258.5 2.2 copy.411
  260.7 3.1 fusion.125
  265.7 1.5 copy.413
  267.2 3.2 all-to-all-start.6
  271.2 29.2 %all-to-all-done.6 = f32[32,8,9,128]{3,1,2,0:T(8,128)S(1)} async-done(((f32[32,8,9,128]{3,1,2,0:T(8,128)}), f32[32,8,9,128]{3,1,2,0:T(8,128)S(1)}, u32[]{:S(2)}, u32[]{:S(2)}) %all-to-all-start.6) | async-done | bytes 1179680 | tf_op jit(solution)/shard_map/all_to_all | solution.py:133
  302.2 11.2 %while.131 = (s32[]{:T(128)}, f32[16,128]{1,0:T(8,128)S(1)}, f32[16,9,9,128]{3,1,2,0:T(8,128)S(1)}, f32[16,9,128]{2,1,0:T(8,128)S(1)}, s32[]{:T(128)}, /*index=5*/s32[]{:T(128)}, s32[]{}) while((s32[]{:T(128)}, f32[16,128]{1,0:T(8,128)S(1)}, f32[16,9,9,128]{3,1,2,0:T(8,128)S(1)}, f32[16,9,128]{2,1,0:T(8,128)S(1)}, s32[]{:T(128)}, ...), condition=%wide.region_24.25_spmd, body=%wide.region_21.24_spmd.sunk | while | flops 2064515 | bytes 1354349 | solution.py:200
  314.7 3.0 all-to-all-start.7
  317.8 8.4 all-to-all-done.7
  327.0 30.2 %while.132 = (s32[]{:T(128)}, f32[16,3,128]{2,0,1:T(8,128)S(1)}, f32[16,128]{1,0:T(8,128)S(1)}, f32[16,9,9,128]{3,1,2,0:T(8,128)S(1)}, f32[16,128]{1,0:T(8,128)S...) while((s32[]{:T(128)}, f32[16,3,128]{2,0,1:T(8,128)S(1)}, ...), condition=%wide.region_30.31_spmd, body=%wide.region_25.30_spmd.sunk | while | flops 7227652 | bytes 4445869 | solution.py:209
  357.3 1.7 gather_fusion.10
  359.1 2.7 all-to-all-start.8
  361.8 16.1 %all-to-all-done.8 = f32[32,8,4,128]{3,2,1,0:T(4,128)S(1)} async-done(((f32[32,8,4,128]{3,2,1,0:T(4,128)}), f32[32,8,4,128]{3,2,1,0:T(4,128)S(1)}, u32[]{:S(2)}, u32[]{:S(2)}) %all-to-all-start.8) | async-done | bytes 524320 | tf_op jit(solution)/shard_map/all_to_all | solution.py:141
  378.9 42.2 %while.133 = (s32[]{:T(128)}, f32[8,16,21,128]{3,2,1,0:T(8,128)S(1)}, f32[8,3,128]{2,1,0:T(4,128)}, f32[8,16,4,128]{3,2,1,0:T(4,128)S(1)}, f32[8,128]{1,0:T(8,12...) while((s32[]{:T(128)}, ...), condition=%wide.region_34.35_spmd, body=%wide.region_31.34_spmd.sunk | while | flops 72364544 | bytes 3670657 | solution.py:220
  422.4 11.7 %scatter_fusion.1 = f32[256,21,128]{2,1,0:T(8,128)S(1)} fusion(f32[256,21,128]{2,1,0:T(8,128)S(1)} %broadcast.472.clone.1, s32[128]{0:T(128)S(1)} %copy-done.42, f32[128,21,128]{2,1,0:T(8,128)} %bitcast.616), kind=kCustom, calls=%fused_computation.27 | custom fusion | bytes 4129280 | tf_op jit(solution)/shard_map/scatter | solution.py:225
  434.7 65.8 %all_to_all.98 = f32[32,8,21,128]{3,1,2,0:T(8,128)S(1)} all-to-all(f32[32,8,21,128]{3,1,2,0:T(8,128)S(1)} %copy.428), channel_id=1, replica_groups=mesh['gx'=4,'gy'=8] {'gx','gy'}, dimensions={0} | all-to-all | bytes 5505024 | tf_op jit(solution)/shard_map/all_to_all | solution.py:145
  500.4 2.2 copy.429
  502.6 3.1 fusion.123
  507.6 1.5 copy.431
  509.1 3.2 all-to-all-start.10
  513.0 29.2 %all-to-all-done.10 = f32[32,8,9,128]{3,1,2,0:T(8,128)S(1)} async-done(((f32[32,8,9,128]{3,1,2,0:T(8,128)}), f32[32,8,9,128]{3,1,2,0:T(8,128)S(1)}, u32[]{:S(2)}, u32[]{:S(2)}) %all-to-all-start.10) | async-done | bytes 1179680 | tf_op jit(solution)/shard_map/all_to_all | solution.py:133
  544.0 11.2 %while.134 = (s32[]{:T(128)}, f32[16,128]{1,0:T(8,128)S(1)}, f32[16,9,9,128]{3,1,2,0:T(8,128)S(1)}, f32[16,9,128]{2,1,0:T(8,128)S(1)}, s32[]{:T(128)}, /*index=5*/s32[]{:T(128)}, s32[]{}) while((s32[]{:T(128)}, f32[16,128]{1,0:T(8,128)S(1)}, f32[16,9,9,128]{3,1,2,0:T(8,128)S(1)}, f32[16,9,128]{2,1,0:T(8,128)S(1)}, s32[]{:T(128)}, ...), condition=%wide.region_39.40_spmd, body=%wide.region_36.39_spmd.sunk | while | flops 2064515 | bytes 1354349 | solution.py:200
  556.5 3.0 all-to-all-start.11
  559.6 8.4 all-to-all-done.11
  568.8 30.2 %while.135 = (s32[]{:T(128)}, f32[16,3,128]{2,0,1:T(8,128)S(1)}, f32[16,128]{1,0:T(8,128)S(1)}, f32[16,9,9,128]{3,1,2,0:T(8,128)S(1)}, f32[16,128]{1,0:T(8,128)S...) while((s32[]{:T(128)}, f32[16,3,128]{2,0,1:T(8,128)S(1)}, ...), condition=%wide.region_45.46_spmd, body=%wide.region_40.45_spmd.sunk | while | flops 7227652 | bytes 4445869 | solution.py:209
  599.2 1.7 gather_fusion.16
  600.9 2.7 all-to-all-start.12
  603.7 16.1 %all-to-all-done.12 = f32[32,8,4,128]{3,2,1,0:T(4,128)S(1)} async-done(((f32[32,8,4,128]{3,2,1,0:T(4,128)}), f32[32,8,4,128]{3,2,1,0:T(4,128)S(1)}, u32[]{:S(2)}, u32[]{:S(2)}) %all-to-all-start.12) | async-done | bytes 524320 | tf_op jit(solution)/shard_map/all_to_all | solution.py:141
  620.8 42.0 %while.136 = (s32[]{:T(128)}, f32[8,16,21,128]{3,2,1,0:T(8,128)S(1)}, f32[8,3,128]{2,1,0:T(4,128)}, f32[8,16,4,128]{3,2,1,0:T(4,128)S(1)}, f32[8,128]{1,0:T(8,12...) while((s32[]{:T(128)}, ...), condition=%wide.region_49.50_spmd, body=%wide.region_46.49_spmd.sunk | while | flops 72364544 | bytes 3670657 | solution.py:220
  664.1 11.7 %scatter_fusion.2 = f32[256,21,128]{2,1,0:T(8,128)S(1)} fusion(f32[256,21,128]{2,1,0:T(8,128)S(1)} %broadcast.472.clone.2, s32[128]{0:T(128)S(1)} %copy-done.43, f32[128,21,128]{2,1,0:T(8,128)} %bitcast.617), kind=kCustom, calls=%fused_computation.28 | custom fusion | bytes 4129280 | tf_op jit(solution)/shard_map/scatter | solution.py:225
  676.4 65.8 %all_to_all.99 = f32[32,8,21,128]{3,1,2,0:T(8,128)S(1)} all-to-all(f32[32,8,21,128]{3,1,2,0:T(8,128)S(1)} %copy.446), channel_id=1, replica_groups=mesh['gx'=4,'gy'=8] {'gx','gy'}, dimensions={0} | all-to-all | bytes 5505024 | tf_op jit(solution)/shard_map/all_to_all | solution.py:145
  742.1 2.2 copy.447
  744.4 3.1 fusion.121
  749.4 1.5 copy.449
  750.9 3.2 all-to-all-start.14
  754.7 29.2 %all-to-all-done.14 = f32[32,8,9,128]{3,1,2,0:T(8,128)S(1)} async-done(((f32[32,8,9,128]{3,1,2,0:T(8,128)}), f32[32,8,9,128]{3,1,2,0:T(8,128)S(1)}, u32[]{:S(2)}, u32[]{:S(2)}) %all-to-all-start.14) | async-done | bytes 1179680 | tf_op jit(solution)/shard_map/all_to_all | solution.py:133
  785.7 11.2 %while.137 = (s32[]{:T(128)}, f32[16,128]{1,0:T(8,128)S(1)}, f32[16,9,9,128]{3,1,2,0:T(8,128)S(1)}, f32[16,9,128]{2,1,0:T(8,128)S(1)}, s32[]{:T(128)}, /*index=5*/s32[]{:T(128)}, s32[]{}) while((s32[]{:T(128)}, f32[16,128]{1,0:T(8,128)S(1)}, f32[16,9,9,128]{3,1,2,0:T(8,128)S(1)}, f32[16,9,128]{2,1,0:T(8,128)S(1)}, s32[]{:T(128)}, ...), condition=%wide.region_54.55_spmd, body=%wide.region_51.54_spmd.sunk | while | flops 2064515 | bytes 1354349 | solution.py:200
  798.3 3.0 all-to-all-start.15
  801.3 8.4 all-to-all-done.15
  810.5 30.2 %while.138 = (s32[]{:T(128)}, f32[16,3,128]{2,0,1:T(8,128)S(1)}, f32[16,128]{1,0:T(8,128)S(1)}, f32[16,9,9,128]{3,1,2,0:T(8,128)S(1)}, f32[16,128]{1,0:T(8,128)S...) while((s32[]{:T(128)}, f32[16,3,128]{2,0,1:T(8,128)S(1)}, ...), condition=%wide.region_60.61_spmd, body=%wide.region_55.60_spmd.sunk | while | flops 7227652 | bytes 4445869 | solution.py:209
  841.9 18.0 %all_to_all.100 = f32[32,8,4,128]{3,2,1,0:T(4,128)S(1)} all-to-all(f32[32,8,4,128]{3,2,1,0:T(4,128)S(1)} %bitcast.639), channel_id=1, replica_groups=mesh['gx'=4,'gy'=8] {'gx','gy'}, dimensions={0} | all-to-all | bytes 1048576 | tf_op jit(solution)/shard_map/all_to_all | solution.py:141
  860.9 42.0 %while.139 = (s32[]{:T(128)}, f32[8,16,21,128]{3,2,1,0:T(8,128)S(1)}, f32[8,3,128]{2,1,0:T(4,128)}, f32[8,16,4,128]{3,2,1,0:T(4,128)S(1)}, f32[8,128]{1,0:T(8,12...) while((s32[]{:T(128)}, ...), condition=%wide.region_64.65_spmd, body=%wide.region_61.64_spmd.sunk | while | flops 72364544 | bytes 3670657 | solution.py:220
  904.3 11.7 %scatter_fusion.3 = f32[256,21,128]{2,1,0:T(8,128)S(1)} fusion(f32[256,21,128]{2,1,0:T(8,128)S(1)} %broadcast.472, s32[128]{0:T(128)S(1)} %copy-done.44, f32[128,21,128]{2,1,0:T(8,128)} %bitcast.618), kind=kCustom, calls=%fused_computation.29 | custom fusion | bytes 4129280 | tf_op jit(solution)/shard_map/scatter | solution.py:225
  916.5 66.3 %all_to_all.101 = f32[32,8,21,128]{3,1,2,0:T(8,128)} all-to-all(f32[32,8,21,128]{3,1,2,0:T(8,128)S(1)} %copy.464), channel_id=1, replica_groups=mesh['gx'=4,'gy'=8] {'gx','gy'}, dimensions={0} | all-to-all | bytes 5505024 | tf_op jit(solution)/shard_map/all_to_all | solution.py:145
  982.8 2.2 copy.465
  (2325 shorter events, 362.9 us)
Async XLA Ops:
  3.4 174.7 %copy-start.41 = (s32[128]{0:T(128)}, s32[128]{0:T(128)S(1)}, u32[]{:S(2)}) copy-start(s32[128]{0:T(128)S(1)} %fusion.148) | copy-start | bytes 1540
  5.1 13.8 %all-to-all-start.3 = ((s32[32,1,8]{2,1,0:T(1,128)}), s32[32,1,8]{2,1,0:T(1,128)S(1)}, u32[]{:S(2)}, u32[]{:S(2)}) async-start(s32[32,1,8]{2,1,0:T(1,128)} %bitcast.122), calls=%async_computation.3 | async-start | bytes 32768 | tf_op jit(solution)/shard_map/all_to_all | solution.py:128
  18.9 10.5 %all-to-all-start = ((s32[32,1,8]{2,1,0:T(1,128)}), s32[32,1,8]{2,1,0:T(1,128)S(1)}, u32[]{:S(2)}, u32[]{:S(2)}) async-start(s32[32,1,8]{2,1,0:T(1,128)} %bitcast.111), calls=%async_computation | async-start | bytes 32768 | tf_op jit(solution)/shard_map/all_to_all | solution.py:127
  33.4 3.1 copy-start.51
  33.4 33.0 %all-to-all-start.1 = ((f32[32,8,9,128]{3,1,2,0:T(8,128)}), f32[32,8,9,128]{3,1,2,0:T(8,128)S(1)}, u32[]{:S(2)}, u32[]{:S(2)}) async-start(f32[32,8,9,128]{3,1,2,0:T(8,128)} %copy.395), calls=%async_computation.1 | async-start | bytes 2359296 | tf_op jit(solution)/shard_map/all_to_all | solution.py:133
  36.5 55.8 %copy-start.40 = (s32[1024]{0:T(1024)}, s32[1024]{0:T(1024)S(1)}, u32[]{:S(2)}) copy-start(s32[1024]{0:T(1024)S(1)} %pad_clamp_fusion.2) | copy-start | bytes 12292
  68.3 11.2 %copy-start.30 = (f32[16,128]{1,0:T(8,128)S(1)}, f32[16,128]{1,0:T(8,128)}, u32[]{:S(2)}) copy-start(f32[16,128]{1,0:T(8,128)} %param.45) | copy-start | bytes 24580
  80.9 11.4 %all-to-all-start.2 = ((f32[32,8,128]{2,1,0:T(8,128)}), f32[32,8,128]{2,1,0:T(8,128)S(1)}, u32[]{:S(2)}, u32[]{:S(2)}) async-start(f32[32,8,128]{2,1,0:T(8,128)} %bitcast.117), calls=%async_computation.2 | async-start | bytes 262144 | tf_op jit(solution)/shard_map/all_to_all | solution.py:137
  93.0 30.3 %copy-start.21 = (f32[16,3,128]{2,0,1:T(8,128)S(1)}, f32[16,3,128]{2,0,1:T(8,128)}, u32[]{:S(2)}) copy-start(f32[16,3,128]{2,0,1:T(8,128)} %param.42) | copy-start | bytes 73732
  93.0 30.3 %copy-start.28 = (f32[16,3,128]{2,0,1:T(8,128)S(1)}, f32[16,3,128]{2,0,1:T(8,128)}, u32[]{:S(2)}) copy-start(f32[16,3,128]{2,0,1:T(8,128)} %param.41) | copy-start | bytes 73732
  93.0 30.4 %copy-start.10 = (f32[16,128]{1,0:T(8,128)S(1)}, f32[16,128]{1,0:T(8,128)}, u32[]{:S(2)}) copy-start(f32[16,128]{1,0:T(8,128)} %param.44) | copy-start | bytes 24580
  123.2 5.0 copy-start.45
  123.3 5.0 copy-start.46
  125.2 20.1 %copy-start.11 = (f32[8,16,128]{2,1,0:T(8,128)S(1)}, f32[8,16,128]{2,1,0:T(8,128)}, u32[]{:S(2)}) copy-start(f32[8,16,128]{2,1,0:T(8,128)} %param.55) | copy-start | bytes 196612
  125.2 19.2 %all-to-all-start.4 = ((f32[32,8,4,128]{3,2,1,0:T(4,128)}), f32[32,8,4,128]{3,2,1,0:T(4,128)S(1)}, u32[]{:S(2)}, u32[]{:S(2)}) async-start(f32[32,8,4,128]{3,2,1,0:T(4,128)} %bitcast.124), calls=%async_computation.4 | async-start | bytes 1048576 | tf_op jit(solution)/shard_map/all_to_all | solution.py:141
  128.3 17.0 %copy-start.47 = (s32[1024]{0:T(1024)}, s32[1024]{0:T(1024)S(1)}, u32[]{:S(2)}) copy-start(s32[1024]{0:T(1024)S(1)} %pad_clamp_fusion) | copy-start | bytes 12292
  176.7 1.2 copy-start
  176.8 13.1 %copy-start.25 = (f32[8,3,128]{2,1,0:T(4,128)}, f32[8,3,128]{2,1,0:T(4,128)S(1)}, u32[]{:S(2)}) copy-start(f32[8,3,128]{2,1,0:T(4,128)S(1)} %get-tuple-element.2125) | copy-start | bytes 36868
  191.9 66.6 %all-to-all-start.5 = ((f32[32,8,21,128]{3,1,2,0:T(8,128)}), f32[32,8,21,128]{3,1,2,0:T(8,128)S(1)}, u32[]{:S(2)}, u32[]{:S(2)}) async-start(f32[32,8,21,128]{3,1,2,0:T(8,128)} %copy.410), calls=%async_computation.5 | async-start | bytes 5505024 | tf_op jit(solution)/shard_map/all_to_all | solution.py:145
  194.9 65.9 %copy-start.36 = (s32[256]{0:T(256)}, s32[256]{0:T(256)S(1)}, u32[]{:S(2)}) copy-start(s32[256]{0:T(256)S(1)} %eq.82) | copy-start | bytes 3076
  260.7 3.1 copy-start.26
  263.9 0.8 copy-start.4
  264.7 1.1 copy-start.12
  267.2 3.3 copy-start.13
  267.2 33.2 %all-to-all-start.6 = ((f32[32,8,9,128]{3,1,2,0:T(8,128)}), f32[32,8,9,128]{3,1,2,0:T(8,128)S(1)}, u32[]{:S(2)}, u32[]{:S(2)}) async-start(f32[32,8,9,128]{3,1,2,0:T(8,128)} %copy.413), calls=%async_computation.6 | async-start | bytes 2359296 | tf_op jit(solution)/shard_map/all_to_all | solution.py:133
  300.8 1.2 copy-start.18
  302.2 11.2 %copy-start.33 = (f32[16,128]{1,0:T(8,128)S(1)}, f32[16,128]{1,0:T(8,128)}, u32[]{:S(2)}) copy-start(f32[16,128]{1,0:T(8,128)} %get-tuple-element.1080) | copy-start | bytes 24580
  314.7 11.4 %all-to-all-start.7 = ((f32[32,8,128]{2,1,0:T(8,128)}), f32[32,8,128]{2,1,0:T(8,128)S(1)}, u32[]{:S(2)}, u32[]{:S(2)}) async-start(f32[32,8,128]{2,1,0:T(8,128)} %bitcast.142), calls=%async_computation.7 | async-start | bytes 262144 | tf_op jit(solution)/shard_map/all_to_all | solution.py:137
  327.0 30.3 %copy-start.49 = (f32[16]{0:T(128)S(1)}, f32[16]{0:T(128)}, u32[]{:S(2)}) copy-start(f32[16]{0:T(128)} %get-tuple-element.1143) | copy-start | bytes 196
  357.3 21.6 %copy-start.22 = (f32[16,3,128]{2,0,1:T(8,128)}, f32[16,3,128]{2,0,1:T(8,128)S(1)}, u32[]{:S(2)}) copy-start(f32[16,3,128]{2,0,1:T(8,128)S(1)} %get-tuple-element.1078) | copy-start | bytes 73732
  359.1 18.8 %all-to-all-start.8 = ((f32[32,8,4,128]{3,2,1,0:T(4,128)}), f32[32,8,4,128]{3,2,1,0:T(4,128)S(1)}, u32[]{:S(2)}, u32[]{:S(2)}) async-start(f32[32,8,4,128]{3,2,1,0:T(4,128)} %bitcast.145), calls=%async_computation.8 | async-start | bytes 1048576 | tf_op jit(solution)/shard_map/all_to_all | solution.py:141
  421.1 1.2 copy-start.1
  421.1 1.4 copy-start.42
  500.4 2.2 copy-start.37
  506.5 1.1 copy-start.14
  506.5 48.6 %copy-start.31 = (f32[16,128]{1,0:T(8,128)}, f32[16,128]{1,0:T(8,128)S(1)}, u32[]{:S(2)}) copy-start(f32[16,128]{1,0:T(8,128)S(1)} %get-tuple-element.1074) | copy-start | bytes 24580
  509.1 3.2 copy-start.15
  509.1 33.1 %all-to-all-start.10 = ((f32[32,8,9,128]{3,1,2,0:T(8,128)}), f32[32,8,9,128]{3,1,2,0:T(8,128)S(1)}, u32[]{:S(2)}, u32[]{:S(2)}) async-start(f32[32,8,9,128]{3,1,2,0:T(8,128)} %copy.431), calls=%async_computation.10 | async-start | bytes 2359296 | tf_op jit(solution)/shard_map/all_to_all | solution.py:133
  542.6 1.2 copy-start.19
  556.5 11.4 %all-to-all-start.11 = ((f32[32,8,128]{2,1,0:T(8,128)}), f32[32,8,128]{2,1,0:T(8,128)S(1)}, u32[]{:S(2)}, u32[]{:S(2)}) async-start(f32[32,8,128]{2,1,0:T(8,128)} %bitcast.163), calls=%async_computation.11 | async-start | bytes 262144 | tf_op jit(solution)/shard_map/all_to_all | solution.py:137
  568.8 30.3 %copy-start.23 = (f32[16,3,128]{2,0,1:T(8,128)S(1)}, f32[16,3,128]{2,0,1:T(8,128)}, u32[]{:S(2)}) copy-start(f32[16,3,128]{2,0,1:T(8,128)} %copy-done.22) | copy-start | bytes 73732
  568.8 30.3 %copy-start.24 = (f32[16,3,128]{2,0,1:T(8,128)S(1)}, f32[16,3,128]{2,0,1:T(8,128)}, u32[]{:S(2)}) copy-start(f32[16,3,128]{2,0,1:T(8,128)} %get-tuple-element.1076) | copy-start | bytes 73732
  568.8 30.3 %copy-start.48 = (f32[16]{0:T(128)S(1)}, f32[16]{0:T(128)}, u32[]{:S(2)}) copy-start(f32[16]{0:T(128)} %get-tuple-element.1142) | copy-start | bytes 196
  600.9 18.9 %all-to-all-start.12 = ((f32[32,8,4,128]{3,2,1,0:T(4,128)}), f32[32,8,4,128]{3,2,1,0:T(4,128)S(1)}, u32[]{:S(2)}, u32[]{:S(2)}) async-start(f32[32,8,4,128]{3,2,1,0:T(4,128)} %bitcast.166), calls=%async_computation.12 | async-start | bytes 1048576 | tf_op jit(solution)/shard_map/all_to_all | solution.py:141
  662.8 1.2 copy-start.2
  662.8 1.4 copy-start.43
  742.1 2.2 copy-start.38
  744.4 3.2 copy-start.32
  747.5 0.8 copy-start.8
  748.3 1.1 copy-start.16
  750.9 3.2 copy-start.17
  750.9 33.1 %all-to-all-start.14 = ((f32[32,8,9,128]{3,1,2,0:T(8,128)}), f32[32,8,9,128]{3,1,2,0:T(8,128)S(1)}, u32[]{:S(2)}, u32[]{:S(2)}) async-start(f32[32,8,9,128]{3,1,2,0:T(8,128)} %copy.449), calls=%async_computation.14 | async-start | bytes 2359296 | tf_op jit(solution)/shard_map/all_to_all | solution.py:133
  784.3 1.2 copy-start.20
  785.7 11.2 %copy-start.34 = (f32[16,128]{1,0:T(8,128)S(1)}, f32[16,128]{1,0:T(8,128)}, u32[]{:S(2)}) copy-start(f32[16,128]{1,0:T(8,128)} %get-tuple-element.1068) | copy-start | bytes 24580
  798.3 11.4 %all-to-all-start.15 = ((f32[32,8,128]{2,1,0:T(8,128)}), f32[32,8,128]{2,1,0:T(8,128)S(1)}, u32[]{:S(2)}, u32[]{:S(2)}) async-start(f32[32,8,128]{2,1,0:T(8,128)} %bitcast.184), calls=%async_computation.15 | async-start | bytes 262144 | tf_op jit(solution)/shard_map/all_to_all | solution.py:137
  810.5 30.3 %copy-start.50 = (f32[16]{0:T(128)S(1)}, f32[16]{0:T(128)}, u32[]{:S(2)}) copy-start(f32[16]{0:T(128)} %get-tuple-element.1065) | copy-start | bytes 196
  840.8 20.0 %copy-start.29 = (f32[16,3,128]{2,0,1:T(8,128)}, f32[16,3,128]{2,0,1:T(8,128)S(1)}, u32[]{:S(2)}) copy-start(f32[16,3,128]{2,0,1:T(8,128)S(1)} %multiply_add_fusion) | copy-start | bytes 73732
  902.9 1.2 copy-start.3
  902.9 1.4 copy-start.44
  982.8 2.3 copy-start.39
  985.0 1.4 copy-start.5
  985.0 1.4 copy-start.7
  985.0 1.4 copy-start.9
  985.0 1.4 copy-start.27
  (2 other events, 1.5 us)
where the time goes:
time: 1000 us; the launch traced here: 989 us
  waiting for transfers between devices  267 us (27%)
  other arithmetic  246 us (25%)
  blocking collectives  216 us (22%)
  local copies, waits for them, and re-layouts  145 us (14%)
  matrix products  51.7 us (5%)
  starting transfers between devices  47 us (5%)
  loops' own time  14.4 us (1%)
    all_to_all x3, blocking collectives, trade_deposits(): lax.all_to_all(payload, ('gx', 'gy'), split_axis=0, concat_axis=0, tiled=...  198 us
    all_to_all x4, waiting for transfers between devices, trade_ghosts(): lax.all_to_all(payload, ('gx', 'gy'), split_axis=0, concat_axis=0, tiled=...  117 us
    all_to_all x1, waiting for transfers between devices, trade_deposits(): lax.all_to_all(payload, ('gx', 'gy'), split_axis=0, concat_axis=0, tiled=...  63.6 us
    all_to_all x3, waiting for transfers between devices, trade_places(): lax.all_to_all(payload, ('gx', 'gy'), split_axis=0, concat_axis=0, tiled=...  47.7 us
    scatter x4, local copies, waits for them, and re-layouts, local(): outgoing.at[star_places]  46.8 us
    dot_general x32, matrix products, star_deposit(): jnp.einsum('qs,lsg->lqg', payload, share, precision=lax.Precision.HIGHEST)  41 us
    reduce_sum x64, other arithmetic, block_force(): converge = jnp.sum(velocity_gap * offset, axis=1)  35.4 us
    all_to_all x4, waiting for transfers between devices, trade_terms(): lax.all_to_all(payload, ('gx', 'gy'), split_axis=0, concat_axis=0, tiled=...  32.7 us
  transfers between devices with their start and end apart: 14, of which 14 were waited for; matrix products, arithmetic and copies ran while one was open for 1% of the time, Pallas kernels for 0%

commit v1 on v0

v1 whole, which is shorter than its diff:
```python
import jax
import jax.numpy as jnp
from jax import lax
from jax.experimental import pallas as pl
from jax.experimental.pallas import tpu as pltpu
from jax.sharding import PartitionSpec as P

SUBSTEPS = 4
KERNEL_NORM = 0.1795871221251666
GAMMA_LESS = 0.6666666666666666
TIME_STEP = 0.05
COOL_RATE = 0.4
ENERGY_FLOOR = 0.2
LOG2E = 1.4426950408889634
AXES = ("gx", "gy")
F32 = jnp.float32
BF16 = jnp.bfloat16
UNROLL = 4
VMEM = pl.BlockSpec(memory_space=pltpu.VMEM)
SMEM = pl.BlockSpec(memory_space=pltpu.SMEM)
PARAMS = pltpu.CompilerParams(vmem_limit_bytes=48 * 1024 * 1024)


def call(body, outs, ins, scratch=(), smem_outs=()):
    return pl.pallas_call(
        body,
        out_shape=[jax.ShapeDtypeStruct(shape, dtype) for shape, dtype in outs],
        in_specs=ins,
        out_specs=[SMEM if at in smem_outs else VMEM for at in range(len(outs))],
        scratch_shapes=list(scratch),
        compiler_params=PARAMS,
    )


def swap(payload):
    return lax.all_to_all(payload, AXES, split_axis=0, concat_axis=0, tiled=True)


def row_of(ref, at):
    return ref[pl.ds(at, 1), :]


def rows8(*rows):
    place = lax.broadcasted_iota(jnp.int32, (8, 128), 0)
    out = jnp.zeros((8, 128), F32)
    for at, row in enumerate(rows):
        out = jnp.where(place == at, row, out)
    return out


def split3(value):
    first = value.astype(BF16).astype(F32)
    rest = value - first
    second = rest.astype(BF16).astype(F32)
    third = (rest - second).astype(BF16).astype(F32)
    return first, second, third


def far_side(value):
    a, b, c = split3(value)
    return jnp.concatenate([a, a, b, b, a, c], axis=0).astype(BF16)


def near_side(value):
    a, b, c = split3(value)
    return jnp.concatenate([a, b, a, b, c, a], axis=0).T.astype(BF16)


def weights(value):
    a, b, c = split3(value)
    packed = jnp.concatenate([a, b, c, jnp.zeros_like(a)], axis=0).astype(BF16)
    return jnp.concatenate([packed, packed], axis=1)


def two_halves(value):
    first = value.astype(BF16)
    second = (value - first.astype(F32)).astype(BF16)
    return jnp.concatenate([first, second], axis=1)


def inner(left, right):
    return lax.dot_general(left, right, (((1,), (1,)), ((), ())), preferred_element_type=F32)


def outer(left, right):
    return lax.dot_general(left, right, (((1,), (0,)), ((), ())), preferred_element_type=F32)


def norm_sq(x, y, z):
    return x * x + y * y + z * z


def plan_kernel(peers, cap, sb, neighbours, entries):
    span = cap + sb

    def body(gas_dev, gas_slot, star_dev, star_slot, req, place, count):
        def clear(at, _):
            req[at] = -1
            return 0

        def clear_count(at, _):
            count[at] = 0
            return 0

        lax.fori_loop(0, peers * span, clear, 0, unroll=8)
        lax.fori_loop(0, peers, clear_count, 0, unroll=8)

        def gas(at, _):
            dev = gas_dev[at]
            used = count[dev]
            count[dev] = used + 1
            req[dev * span + used] = gas_slot[at]
            place[at] = dev * cap + used
            return 0

        def star(at, _):
            req[star_dev[at] * span + cap + at // entries] = star_slot[at]
            return 0

        lax.fori_loop(0, gas_dev.shape[0], gas, 0, unroll=4)
        lax.fori_loop(0, star_dev.shape[0], star, 0, unroll=4)

    return body


def list_kernel(peers, cap, sb, nb):
    span = cap + sb

    def body(asked, pick, list_c, list_slot, list_out, number):
        def picks(at, _):
            pick[at] = jnp.maximum(asked[(at // cap) * span + at % cap], 0)
            return 0

        lax.fori_loop(0, peers * cap, picks, 0, unroll=8)

        def stars(at, used):
            slot = asked[(at // sb) * span + cap + at % sb]
            list_c[used] = at
            list_slot[used] = slot
            list_out[used] = at
            return used + jnp.where(slot >= 0, 1, 0)

        used = lax.fori_loop(0, peers * sb, stars, 0, unroll=4)
        for extra in range(UNROLL):
            list_c[used + extra] = 0
            list_slot[used + extra] = nb
            list_out[used + extra] = peers * sb
        number[0] = (used + UNROLL - 1) // UNROLL

    return body


def send_rows(pick, out, source, width):
    total = out.shape[0] // width

    def one(at, _):
        slot = pick[at]
        for f in range(width):
            out[pl.ds(at * width + f, 1), :] = source(slot, f)
        return 0

    lax.fori_loop(0, total, one, 0, unroll=8)


def start_kernel(pick, pos, vel, mass, smooth, send_pos, send_vel, send_mass, send_smooth):
    send_rows(pick, send_pos, lambda slot, f: pos[slot, f : f + 1, :], 3)
    send_rows(pick, send_vel, lambda slot, f: vel[slot, f : f + 1, :], 3)
    send_rows(pick, send_mass, lambda slot, f: row_of(mass, slot), 1)
    send_rows(pick, send_smooth, lambda slot, f: row_of(smooth, slot), 1)


def density_kernel(neighbours):
    def body(place, pick, pos, vel, mass, smooth, energy, far_pos, far_vel, far_mass, sums, term, gain, density, send_gain):
        def block(b, _):
            x, y, z = (pos[b, f : f + 1, :] for f in range(3))
            h = row_of(smooth, b)
            scale = LOG2E / (h * h)
            near = near_side(
                rows8(2.0 * scale * x, 2.0 * scale * y, 2.0 * scale * z, -scale, -scale * norm_sq(x, y, z))
            )

            def pair(px, py, pz, vx, vy, vz, m):
                far = far_side(rows8(px, py, pz, norm_sq(px, py, pz), 1.0))
                reach = jnp.exp2(outer(near, far))
                load = rows8(
                    m, m * px, m * py, m * pz, m * vx, m * vy, m * vz, m * (px * vx + py * vy + pz * vz)
                )
                return inner(weights(load), two_halves(reach))

            total = pair(x, y, z, *(vel[b, f : f + 1, :] for f in range(3)), row_of(mass, b))
            for k in range(neighbours):
                at = place[b * neighbours + k]
                total = total + pair(
                    *(row_of(far_pos, at * 3 + f) for f in range(3)),
                    *(row_of(far_vel, at * 3 + f) for f in range(3)),
                    row_of(far_mass, at),
                )
            total = total[0:8] + total[8:16] + total[16:24]
            sums[b] = total
            dense = KERNEL_NORM * total[0:1] / (h * h * h)
            density[pl.ds(b, 1), :] = dense
            own = GAMMA_LESS * row_of(energy, b) / dense
            term[pl.ds(b, 1), :] = own
            gain[pl.ds(b, 1), :] = row_of(mass, b) * own * ((2.0 * KERNEL_NORM) / (h * h * h * h * h))
            return 0

        lax.fori_loop(0, pos.shape[0], block, 0)
        send_rows(pick, send_gain, lambda slot, f: row_of(gain, slot), 1)

    return body


def force_kernel(neighbours, substep):
    def body(
        place, pick, bins, pos, vel, smooth, energy, term, gain, sums, far_pos, far_smooth, far_gain,
        new_pos, new_vel, new_energy, send_pos,
    ):
        def block(b, _):
            period = jnp.left_shift(1, bins[b])
            active = (substep & (period - 1)) == 0
            x, y, z = (pos[b, f : f + 1, :] for f in range(3))
            u, v, w = (vel[b, f : f + 1, :] for f in range(3))

            @pl.when(active)
            def _():
                h = row_of(smooth, b)
                own = row_of(term, b)
                near = near_side(rows8(2.0 * x, 2.0 * y, 2.0 * z, -1.0, -norm_sq(x, y, z)))

                def pair(px, py, pz, width, push):
                    scale = LOG2E / (width * width)
                    far = far_side(rows8(scale * px, scale * py, scale * pz, scale * norm_sq(px, py, pz), scale))
                    reach = jnp.exp2(outer(near, far))
                    load = rows8(push, push * px, push * py, push * pz)
                    return inner(weights(load), two_halves(reach))

                total = pair(x, y, z, h, row_of(gain, b))

                for k in range(neighbours):
                    at = place[b * neighbours + k]
                    total = total + pair(
                        *(row_of(far_pos, at * 3 + f) for f in range(3)), row_of(far_smooth, at), row_of(far_gain, at)
                    )
                total = total[0:8] + total[8:16] + total[16:24]
                near_sum = sums[b]
                grad = own * ((2.0 * KERNEL_NORM) / (h * h * h * h * h))
                kick = TIME_STEP * period.astype(F32)
                acc = []
                for f, place_f in enumerate((x, y, z)):
                    one = grad * (place_f * near_sum[0:1] - near_sum[f + 1 : f + 2])
                    two = place_f * total[0:1] - total[f + 1 : f + 2]
                    acc.append(one + two)
                heat = (
                    (x * u + y * v + z * w) * near_sum[0:1]
                    - (u * near_sum[1:2] + v * near_sum[2:3] + w * near_sum[3:4])
                    - (x * near_sum[4:5] + y * near_sum[5:6] + z * near_sum[6:7])
                    + near_sum[7:8]
                )
                new_energy[pl.ds(b, 1), :] = row_of(energy, b) - kick * (grad * heat)
                for f, (speed, place_f) in enumerate(((u, x), (v, y), (w, z))):
                    now = speed + kick * acc[f]
                    new_vel[b, f : f + 1, :] = now
                    new_pos[b, f : f + 1, :] = place_f + TIME_STEP * now

            @pl.when(jnp.logical_not(active))
            def _():
                new_energy[pl.ds(b, 1), :] = row_of(energy, b)
                new_vel[b] = vel[b]
                new_pos[b] = pos[b] + TIME_STEP * vel[b]

            return 0

        lax.fori_loop(0, pos.shape[0], block, 0)
        send_rows(pick, send_pos, lambda slot, f: new_pos[slot, f : f + 1, :], 3)

    return body


def gas_sides(pos, sides):
    def one(b, _):
        x, y, z = (pos[b, f : f + 1, :] for f in range(3))
        sides[b] = near_side(rows8(-2.0 * x, -2.0 * y, -2.0 * z, 1.0, norm_sq(x, y, z)))
        return 0

    blocks = pos.shape[0]
    lax.fori_loop(0, blocks, one, 0)
    sides[blocks] = jnp.zeros(sides.shape[1:], BF16)


def omega_of(star, c, when, sides, widths, slot):
    x, y, z = (star[c, f : f + 1, :] + when * star[c, f + 3 : f + 4, :] for f in range(3))
    far = far_side(rows8(x, y, z, norm_sq(x, y, z), 1.0))
    dist_sq = jnp.maximum(outer(sides[slot], far), 1e-30)
    wide = dist_sq + widths[slot]
    return (1.0 - dist_sq * lax.rsqrt(dist_sq * wide)) * jnp.exp2(dist_sq * star[c, 6:7, :])


def omega_kernel(substep):
    when = (substep + 1) * TIME_STEP

    def body(list_c, list_slot, list_out, number, pos, widths, star, part, sides, room):
        gas_sides(pos, sides)
        room[...] = jnp.zeros_like(room)

        def group(at, _):
            for lane in range(UNROLL):
                e = at * UNROLL + lane
                omega = omega_of(star, list_c[e], when, sides, widths, list_slot[e])
                room[pl.ds(list_out[e], 1), :] = jnp.sum(omega, axis=0, keepdims=True)
            return 0

        lax.fori_loop(0, number[0], group, 0)
        part[...] = room[0 : part.shape[0], :]

    return body


def deposit_kernel(substep, last):
    when = (substep + 1) * TIME_STEP

    def body(
        list_c, list_slot, number, pick, pos, widths, star, pay, total, mass, vel, energy, metals, density, *rest
    ):
        if last:
            new_mass, new_vel, new_energy, new_metals, sides, dep = rest
        else:
            new_mass, new_vel, new_energy, new_metals, send_mass, send_vel, sides, dep = rest
        gas_sides(pos, sides)
        dep[...] = jnp.zeros_like(dep)

        def group(at, _):
            parts = []
            for lane in range(UNROLL):
                e = at * UNROLL + lane
                c, slot = list_c[e], list_slot[e]
                omega = two_halves(omega_of(star, c, when, sides, widths, slot))
                load = pay[c] * (1.0 / row_of(total, c))
                first = load.astype(BF16).astype(F32)
                left = jnp.concatenate([first, load - first], axis=0).astype(BF16)
                out = inner(jnp.concatenate([left, left], axis=1), omega)
                parts.append((slot, out[0:24] + out[24:48]))
            for slot, out in parts:
                dep[slot] = dep[slot] + out
            return 0

        lax.fori_loop(0, number[0], group, 0)

        def block(b, _):
            got = dep[b]
            m = row_of(mass, b)
            grown = m + got[0:1]
            new_mass[pl.ds(b, 1), :] = grown
            new_vel[b] = (m * vel[b] + got[1:4]) / grown
            cooled = ENERGY_FLOOR + (row_of(energy, b) - ENERGY_FLOOR) * jnp.exp(
                (-TIME_STEP * COOL_RATE) * row_of(density, b)
            )
            new_energy[pl.ds(b, 1), :] = (m * cooled + got[4:5]) / grown
            new_metals[b] = metals[b] + got[8:24]
            return 0

        lax.fori_loop(0, pos.shape[0], block, 0)
        if not last:
            send_rows(pick, send_mass, lambda slot, f: row_of(new_mass, slot), 1)
            send_rows(pick, send_vel, lambda slot, f: new_vel[slot, f : f + 1, :], 3)

    return body


def local(
    gas_pos, gas_vel, gas_mass, gas_smooth, gas_energy, gas_metals, gas_bins, gas_nbr_dev, gas_nbr_slot,
    star_pos, star_vel, star_radius, star_mdot, star_edot, star_yields, star_ovl_dev, star_ovl_slot,
):
    peers = lax.axis_size(AXES)
    nb, neighbours = gas_nbr_dev.shape
    sb, entries = star_ovl_dev.shape
    width = gas_pos.shape[2]
    loads = 24
    cap = max(2, 2 * nb * neighbours // peers)
    span = cap + sb
    stars = peers * sb
    sent = peers * cap
    i32 = jnp.int32

    with jax.named_scope("star_data"):
        ejecta = star_mdot * TIME_STEP
        reach = -LOG2E / (star_radius * star_radius)
        star8 = jnp.concatenate([star_pos, star_vel, reach[:, None], jnp.zeros_like(reach)[:, None]], axis=1)
        pay = jnp.concatenate(
            [
                ejecta[:, None],
                ejecta[:, None] * star_vel,
                (star_edot * TIME_STEP)[:, None],
                jnp.zeros((sb, 3, width), F32),
                ejecta[:, None] * star_yields,
            ],
            axis=1,
        )
        widths = jnp.broadcast_to((gas_smooth * gas_smooth)[:, :, None], (nb, width, width))
        widths = jnp.concatenate([widths, jnp.ones((1, width, width), F32)], axis=0)

    with jax.named_scope("plan"):
        req, place = call(
            plan_kernel(peers, cap, sb, neighbours, entries),
            [((peers * span,), i32), ((nb * neighbours,), i32)],
            [SMEM] * 4,
            [pltpu.SMEM((peers,), i32)],
            smem_outs=(0, 1),
        )(gas_nbr_dev.reshape(-1), gas_nbr_slot.reshape(-1), star_ovl_dev.reshape(-1), star_ovl_slot.reshape(-1))
        asked = swap(req.reshape(peers, span)).reshape(-1)
        pick, list_c, list_slot, list_out, number = call(
            list_kernel(peers, cap, sb, nb),
            [((sent,), i32)] + [((stars + 2 * UNROLL,), i32)] * 3 + [((1,), i32)],
            [SMEM],
            smem_outs=range(5),
        )(asked)

    with jax.named_scope("start"):
        sends = call(
            start_kernel,
            [((sent * 3, width), F32), ((sent * 3, width), F32), ((sent, width), F32), ((sent, width), F32)],
            [SMEM] + [VMEM] * 4,
        )(pick, gas_pos, gas_vel, gas_mass, gas_smooth)
        far_pos, far_vel, far_mass, far_smooth = (swap(one) for one in sends)

    with jax.named_scope("star_share"):
        all_stars = lax.all_gather(jnp.concatenate([star8, pay], axis=1), AXES, axis=0, tiled=True)
        all_star8, all_pay = all_stars[:, 0:8], all_stars[:, 8:32]

    pos, vel, mass, energy, metals = gas_pos, gas_vel, gas_mass, gas_energy, gas_metals
    sides = pltpu.VMEM((nb + 1, width, 48), BF16)
    for substep in range(SUBSTEPS):
        last = substep == SUBSTEPS - 1
        with jax.named_scope("density"):
            sums, term, gain, density, send_gain = call(
                density_kernel(neighbours),
                [((nb, 8, width), F32)] + [((nb, width), F32)] * 3 + [((sent, width), F32)],
                [SMEM] * 2 + [VMEM] * 8,
            )(place, pick, pos, vel, mass, gas_smooth, energy, far_pos, far_vel, far_mass)
            far_gain = swap(send_gain)
        with jax.named_scope("force"):
            pos, vel, energy, send_pos = call(
                force_kernel(neighbours, substep),
                [((nb, 3, width), F32), ((nb, 3, width), F32), ((nb, width), F32), ((sent * 3, width), F32)],
                [SMEM] * 3 + [VMEM] * 10,
            )(place, pick, gas_bins, pos, vel, gas_smooth, energy, term, gain, sums, far_pos, far_smooth, far_gain)
            if not last:
                far_pos = swap(send_pos)
        with jax.named_scope("omega"):
            part = call(
                omega_kernel(substep),
                [((stars, width), F32)],
                [SMEM] * 4 + [VMEM] * 3,
                [sides, pltpu.VMEM((stars + 8, width), F32)],
            )(list_c, list_slot, list_out, number, pos, widths, all_star8)[0]
            totals = jnp.sum(swap(part).reshape(peers, sb, width), axis=0)
            total = swap(jnp.broadcast_to(totals[None], (peers, sb, width)).reshape(stars, width))
        with jax.named_scope("deposit"):
            outs = call(
                deposit_kernel(substep, last),
                [((nb, width), F32), ((nb, 3, width), F32), ((nb, width), F32), ((nb, 16, width), F32)]
                + ([] if last else [((sent, width), F32), ((sent * 3, width), F32)]),
                [SMEM] * 4 + [VMEM] * 10,
                [sides, pltpu.VMEM((nb + 1, loads, width), F32)],
            )(
                list_c, list_slot, number, pick, pos, widths, all_star8, all_pay, total,
                mass, vel, energy, metals, density,
            )
            mass, vel, energy, metals = outs[:4]
            if not last:
                far_mass, far_vel = swap(outs[4]), swap(outs[5])
    return (pos, vel, mass, energy, metals)


def solution(mesh):
    split = [P(AXES, *([None] * (rank - 1))) for rank in (3, 3, 2, 2, 2, 3, 1, 2, 2, 3, 3, 2, 2, 2, 3, 2, 2)]
    return jax.shard_map(
        local,
        mesh=mesh,
        in_specs=tuple(split),
        out_specs=tuple(P(AXES, *([None] * (rank - 1))) for rank in (3, 3, 2, 2, 3)),
        check_vma=False,
    )
```

time: 1000 us -> 707 us (0.71)
  Pallas kernels: 0 us -> 282 us
  waiting for transfers between devices: 267 us -> 20.8 us
  other arithmetic: 246 us -> 4.47 us
  local copies, waits for them, and re-layouts: 145 us -> 28.5 us
  blocking collectives: 216 us -> 325 us
  matrix products: 51.7 us -> 0 us
  starting transfers between devices: 47 us -> 20.4 us
  loops' own time: 14.4 us -> 0 us
  between operations: 2.54 us -> 14.5 us
    pallas_call x0 -> x19, Pallas kernels: none -> 282 us  [the longest x4 120 us: local(): call(deposit_kernel(substep, last), [((nb, width), F32), ((nb, 3, width),...]
    all_to_all x14 -> x5, waiting for transfers between devices: 267 us -> 20.7 us  [swap(): lax.all_to_all(payload, AXES, split_axis=0, concat_axis=0, tiled=True)]
    reduce_sum x386 -> x4, other arithmetic: 145 us -> 0.14 us  [local(): totals = jnp.sum(swap(part).reshape(peers, sb, width), axis=0)]
    all_to_all x4 -> x21, blocking collectives: 216 us -> 325 us  [swap(): lax.all_to_all(payload, AXES, split_axis=0, concat_axis=0, tiled=True)]
    mul x452 -> x5, other arithmetic: 94 us -> 2.95 us  [the longest x1 0.85 us: local(): ejecta[:, None] * star_yields]
    dot_general x36 -> x0, matrix products: 51.7 us -> none  [the longest x32 41 us: star_deposit(): jnp.einsum('qs,lsg->lqg', payload, share, precision=lax.Precision.HIGHEST)]
    scatter x6 -> x0, local copies, waits for them, and re-layouts: 48.8 us -> none  [the longest x4 46.8 us: local(): outgoing.at[star_places]]
    gather x28 -> x0, local copies, waits for them, and re-layouts: 31.8 us -> none  [the longest x8 10.1 us: local(): arrived = trade_ghosts(gas_state[gas_pick])]
  transfers between devices with their start and end apart: 14 -> 6, of which waited for: 14 -> 3; matrix products, arithmetic and copies ran while one was open for 1% -> 2% of each run, Pallas kernels for 0% -> 11%
where the time goes in v1:
time: 707 us; the launch traced here: 695 us
  blocking collectives  325 us (46%)
  Pallas kernels  282 us (40%)
  local copies, waits for them, and re-layouts  28.5 us (4%)
  waiting for transfers between devices  20.8 us (3%)
  starting transfers between devices  20.4 us (3%)
  between operations  14.5 us (2%)
    all_to_all x21, blocking collectives, swap(): lax.all_to_all(payload, AXES, split_axis=0, concat_axis=0, tiled=True)  325 us
    pallas_call x4, Pallas kernels, local(): call(deposit_kernel(substep, last), [((nb, width), F32), ((nb, 3, width),...  120 us
    pallas_call x4, Pallas kernels, local(): call(density_kernel(neighbours), [((nb, 8, width), F32)] + [((nb, width),...  63.9 us
    pallas_call x4, Pallas kernels, local(): call(omega_kernel(substep), [((stars, width), F32)], [SMEM] * 4 + [VMEM]...  57.1 us
    pallas_call x4, Pallas kernels, local(): call(force_kernel(neighbours, substep), [((nb, 3, width), F32), ((nb, 3,...  28.8 us
    all_to_all x5, waiting for transfers between devices, swap(): lax.all_to_all(payload, AXES, split_axis=0, concat_axis=0, tiled=True)  20.7 us
    all_to_all x5, starting transfers between devices, swap(): lax.all_to_all(payload, AXES, split_axis=0, concat_axis=0, tiled=True)  20.4 us
    unnamed x77, local copies, waits for them, and re-layouts  17.4 us
  transfers between devices with their start and end apart: 6, of which 3 were waited for; matrix products, arithmetic and copies ran while one was open for 2% of the time, Pallas kernels for 11%

profile of v1, /device:TPU:1, one launch (start us, length us, event | category | flops | bytes accessed | tf_op | source)
XLA Modules:
  0.0 695.3 jit_solution(10107196298632626377)
XLA Ops:
  9.3 0.7 copy.60
  10.0 0.7 broadcast_multiply_fusion.1
  10.7 0.8 broadcast_multiply_fusion
  11.6 1.9 concatenate.7
  13.5 0.8 reshape.104.star_dev
  14.3 0.8 reshape.105.star_slot
  15.1 0.8 copy.50
  15.9 0.8 copy.51
  16.8 3.6 plan.2
  21.0 7.1 %all-to-all-start = ((s32[32,1,16]{2,1,0:T(1,128)}), s32[32,1,16]{2,1,0:T(1,128)S(1)}, u32[]{:S(2)}, u32[]{:S(2)}) async-start(s32[32,1,16]{2,1,0:T(1,128)} %bitcast), calls=%async_computation | async-start | bytes 32768 | tf_op jit(solution)/shard_map/plan/all_to_all | solution.py:36
  28.1 0.8 copy.57.pos
  28.9 0.8 copy.58.vel
  29.7 5.2 all-to-all-done
  36.1 5.9 plan.3
  43.4 2.8 start.1
  46.2 11.0 %all_to_all.264 = f32[32,8,128]{2,1,0:T(8,128)S(1)} all-to-all(f32[32,8,128]{2,1,0:T(8,128)S(1)} %bitcast.93), channel_id=1, replica_groups=mesh['gx'=4,'gy'=8] {'gx','gy'}, dimensions={0} | all-to-all | bytes 262144 | tf_op jit(solution)/shard_map/start/all_to_all | solution.py:36
  57.2 24.5 %all_to_all.265 = f32[32,24,128]{2,1,0:T(8,128)S(1)} all-to-all(f32[32,24,128]{2,1,0:T(8,128)S(1)} %bitcast.86), channel_id=1, replica_groups=mesh['gx'=4,'gy'=8] {'gx','gy'}, dimensions={0} | all-to-all | bytes 786432 | tf_op jit(solution)/shard_map/start/all_to_all | solution.py:36
  81.7 15.7 %all_to_all.266 = f32[32,24,128]{2,1,0:T(8,128)S(1)} all-to-all(f32[32,24,128]{2,1,0:T(8,128)S(1)} %bitcast.85), channel_id=1, replica_groups=mesh['gx'=4,'gy'=8] {'gx','gy'}, dimensions={0} | all-to-all | bytes 786432 | tf_op jit(solution)/shard_map/start/all_to_all | solution.py:36
  97.5 2.6 all-to-all-start.4
  100.1 16.5 %density.4 = (f32[16,8,128]{2,1,0:T(8,128)S(1)}, f32[16,128]{1,0:T(8,128)S(1)}, f32[16,128]{1,0:T(8,128)S(1)}, f32[16,128]{1,0:T(8,128)S(1)}, f32[256,128]{1,0:T(8,128)}) custom-call(s32[128]{0:T(128)S(1)} %get-tuple-element.73.place, s32[256]{0:T(256)S(1)} %get-tuple-element.75.pick, f32[16,3,128]{2,1,0:T(4,128)S(1)} %copy.57.pos, ...), custom_call_target="tpu_custom_call" | custom-call | tf_op jit(solution)/shard_map/density/pallas_call | solution.py:434
  117.2 6.0 all-to-all-start.5
  123.6 7.8 %all-to-all-done.5 = f32[32,8,128]{2,1,0:T(8,128)S(1)} async-done(((f32[32,8,128]{2,1,0:T(8,128)}), f32[32,8,128]{2,1,0:T(8,128)S(1)}, u32[]{:S(2)}, u32[]{:S(2)}) %all-to-all-start.5) | async-done | bytes 131104 | tf_op jit(solution)/shard_map/density/all_to_all | solution.py:36
  131.4 16.6 %force.4 = (f32[16,3,128]{2,1,0:T(4,128)S(1)}, f32[16,3,128]{2,1,0:T(4,128)S(1)}, f32[16,128]{1,0:T(8,128)S(1)}, f32[768,128]{1,0:T(8,128)}) custom-call(s32[128]{0:T(128)S(1)} %get-tuple-element.73.place, s32[256]{0:T(256)S(1)} %get-tuple-element.75.pick, s32[16]{0:T(128)S(1)} %copy-done.31, f32[16,3,128]{2,1,0:T(4,128)S(1)} %copy.57.pos, ...), custom_call_target="tpu_custom_call" | custom-call | tf_op jit(solution)/shard_map/force/pallas_call | solution.py:441
  149.3 1.3 slice.8.star
  150.6 14.3 %omega.4 = f32[256,128]{1,0:T(8,128)S(1)} custom-call(s32[264]{0:T(512)S(1)} %get-tuple-element.85.list_c, s32[264]{0:T(512)S(1)} %get-tuple-element.86.list_slot, s32[264]{0:T(512)S(1)} %get-tuple-element.88.list_out, s32[1]{0:T(128)} %get-tuple-element.87.number, f32[16,3,128]{2,1,0:T(4,128)S(1)} %get-tuple-element.84.pos, ...), custom_call_target="tpu_custom_call" | custom-call | tf_op jit(solution)/shard_map/omega/pallas_call | solution.py:449
  164.9 13.3 %all_to_all.267 = f32[32,8,128]{2,1,0:T(8,128)S(1)} all-to-all(f32[32,8,128]{2,1,0:T(8,128)S(1)} %bitcast.77), channel_id=1, replica_groups=mesh['gx'=4,'gy'=8] {'gx','gy'}, dimensions={0} | all-to-all | bytes 262144 | tf_op jit(solution)/shard_map/omega/all_to_all | solution.py:36
  178.2 9.9 %all_to_all.268 = f32[32,8,128]{2,1,0:T(8,128)S(1)} all-to-all(f32[32,8,128]{2,1,0:T(8,128)S(1)} %broadcast_in_dim.26), channel_id=1, replica_groups=mesh['gx'=4,'gy'=8] {'gx','gy'}, dimensions={0} | all-to-all | bytes 262144 | tf_op jit(solution)/shard_map/omega/all_to_all | solution.py:36
  188.1 2.4 all-to-all-start.8
  190.6 3.8 slice.9.pay
  194.4 30.3 %deposit.4 = (f32[16,128]{1,0:T(8,128)S(1)}, f32[16,3,128]{2,1,0:T(4,128)S(1)}, f32[16,128]{1,0:T(8,128)S(1)}, f32[16,16,128]{2,1,0:T(8,128)S(1)}, f32[256,128]{1,0:T(8,128)S(1)}, /*index=5*/f32[768,128]{1,0:T(8,128)S(1)}) custom-call(s32[264]{0:T(512)S(1)} %get-tuple-element.85.list_c, s32[264]{0:T(512)S(1)} %copy-done.5, s32[1]{0:T(128)} %get-tuple-element.87.number, ...), custom_call_target="tpu_custom_call" | custom-call | tf_op jit(solution)/shard_map/deposit/pallas_call | solution.py:458
  226.0 21.5 %all_to_all.269 = f32[32,8,128]{2,1,0:T(8,128)S(1)} all-to-all(f32[32,8,128]{2,1,0:T(8,128)S(1)} %bitcast.87), channel_id=1, replica_groups=mesh['gx'=4,'gy'=8] {'gx','gy'}, dimensions={0} | all-to-all | bytes 262144 | tf_op jit(solution)/shard_map/deposit/all_to_all | solution.py:36
  247.5 15.2 %all_to_all.270 = f32[32,24,128]{2,1,0:T(8,128)S(1)} all-to-all(f32[32,24,128]{2,1,0:T(8,128)S(1)} %bitcast.82), channel_id=1, replica_groups=mesh['gx'=4,'gy'=8] {'gx','gy'}, dimensions={0} | all-to-all | bytes 786432 | tf_op jit(solution)/shard_map/deposit/all_to_all | solution.py:36
  262.7 0.7 copy-done.15
  264.7 15.8 %density.5 = (f32[16,8,128]{2,1,0:T(8,128)S(1)}, f32[16,128]{1,0:T(8,128)S(1)}, f32[16,128]{1,0:T(8,128)S(1)}, f32[16,128]{1,0:T(8,128)S(1)}, f32[256,128]{1,0:T(8,128)S(1)}) custom-call(s32[128]{0:T(128)S(1)} %copy-done.19, s32[256]{0:T(256)S(1)} %get-tuple-element.75.pick, f32[16,3,128]{2,1,0:T(4,128)S(1)} %get-tuple-element.84.pos, ...), custom_call_target="tpu_custom_call" | custom-call | tf_op jit(solution)/shard_map/density/pallas_call | solution.py:434
  280.5 10.3 %all_to_all.271 = f32[32,8,128]{2,1,0:T(8,128)S(1)} all-to-all(f32[32,8,128]{2,1,0:T(8,128)S(1)} %bitcast.90), channel_id=1, replica_groups=mesh['gx'=4,'gy'=8] {'gx','gy'}, dimensions={0} | all-to-all | bytes 262144 | tf_op jit(solution)/shard_map/density/all_to_all | solution.py:36
  291.5 1.4 force.5
  294.8 14.3 %omega.5 = f32[256,128]{1,0:T(8,128)S(1)} custom-call(s32[264]{0:T(512)S(1)} %get-tuple-element.85.list_c, s32[264]{0:T(512)S(1)} %copy-done.6, s32[264]{0:T(512)S(1)} %copy-done.21, s32[1]{0:T(128)} %get-tuple-element.87.number, f32[16,3,128]{2,1,0:T(4,128)S(1)} %get-tuple-element.102.pos, f32[17,128,128]{2,1,0:T(8,128)S(1)} %concatenate.6.widths, ...), custom_call_target="tpu_custom_call" | custom-call | tf_op jit(solution)/shard_map/omega/pallas_call | solution.py:449
  309.1 22.4 %all_to_all.272 = f32[32,8,128]{2,1,0:T(8,128)S(1)} all-to-all(f32[32,8,128]{2,1,0:T(8,128)S(1)} %bitcast.78), channel_id=1, replica_groups=mesh['gx'=4,'gy'=8] {'gx','gy'}, dimensions={0} | all-to-all | bytes 262144 | tf_op jit(solution)/shard_map/omega/all_to_all | solution.py:36
  331.5 9.9 %all_to_all.273 = f32[32,8,128]{2,1,0:T(8,128)S(1)} all-to-all(f32[32,8,128]{2,1,0:T(8,128)S(1)} %broadcast_in_dim.27), channel_id=1, replica_groups=mesh['gx'=4,'gy'=8] {'gx','gy'}, dimensions={0} | all-to-all | bytes 262144 | tf_op jit(solution)/shard_map/omega/all_to_all | solution.py:36
  341.4 0.7 copy-done.30
  342.1 30.3 %deposit.5 = (f32[16,128]{1,0:T(8,128)S(1)}, f32[16,3,128]{2,1,0:T(4,128)S(1)}, f32[16,128]{1,0:T(8,128)S(1)}, f32[16,16,128]{2,1,0:T(8,128)S(1)}, f32[256,128]{1,0:T(8,128)S(1)}, /*index=5*/f32[768,128]{1,0:T(8,128)S(1)}) custom-call(s32[264]{0:T(512)S(1)} %get-tuple-element.85.list_c, s32[264]{0:T(512)S(1)} %copy-done.7, s32[1]{0:T(128)} %get-tuple-element.87.number, ...), custom_call_target="tpu_custom_call" | custom-call | tf_op jit(solution)/shard_map/deposit/pallas_call | solution.py:458
  372.5 18.1 %all_to_all.274 = f32[32,8,128]{2,1,0:T(8,128)S(1)} all-to-all(f32[32,8,128]{2,1,0:T(8,128)S(1)} %bitcast.88), channel_id=1, replica_groups=mesh['gx'=4,'gy'=8] {'gx','gy'}, dimensions={0} | all-to-all | bytes 262144 | tf_op jit(solution)/shard_map/deposit/all_to_all | solution.py:36
  390.6 15.0 %all_to_all.275 = f32[32,24,128]{2,1,0:T(8,128)S(1)} all-to-all(f32[32,24,128]{2,1,0:T(8,128)S(1)} %bitcast.80), channel_id=1, replica_groups=mesh['gx'=4,'gy'=8] {'gx','gy'}, dimensions={0} | all-to-all | bytes 786432 | tf_op jit(solution)/shard_map/force/all_to_all | solution.py:36
  405.6 15.5 %all_to_all.276 = f32[32,24,128]{2,1,0:T(8,128)S(1)} all-to-all(f32[32,24,128]{2,1,0:T(8,128)S(1)} %bitcast.83), channel_id=1, replica_groups=mesh['gx'=4,'gy'=8] {'gx','gy'}, dimensions={0} | all-to-all | bytes 786432 | tf_op jit(solution)/shard_map/deposit/all_to_all | solution.py:36
  421.2 15.8 %density.6 = (f32[16,8,128]{2,1,0:T(8,128)S(1)}, f32[16,128]{1,0:T(8,128)S(1)}, f32[16,128]{1,0:T(8,128)S(1)}, f32[16,128]{1,0:T(8,128)S(1)}, f32[256,128]{1,0:T(8,128)S(1)}) custom-call(s32[128]{0:T(128)S(1)} %copy-done.19, s32[256]{0:T(256)S(1)} %get-tuple-element.75.pick, f32[16,3,128]{2,1,0:T(4,128)S(1)} %get-tuple-element.102.pos, ...), custom_call_target="tpu_custom_call" | custom-call | tf_op jit(solution)/shard_map/density/pallas_call | solution.py:434
  437.0 10.4 %all_to_all.277 = f32[32,8,128]{2,1,0:T(8,128)S(1)} all-to-all(f32[32,8,128]{2,1,0:T(8,128)S(1)} %bitcast.91), channel_id=1, replica_groups=mesh['gx'=4,'gy'=8] {'gx','gy'}, dimensions={0} | all-to-all | bytes 262144 | tf_op jit(solution)/shard_map/density/all_to_all | solution.py:36
  447.4 8.7 %force.6 = (f32[16,3,128]{2,1,0:T(4,128)S(1)}, f32[16,3,128]{2,1,0:T(4,128)S(1)}, f32[16,128]{1,0:T(8,128)S(1)}, f32[768,128]{1,0:T(8,128)S(1)}) custom-call(s32[128]{0:T(128)S(1)} %copy-done.19, s32[256]{0:T(256)S(1)} %get-tuple-element.75.pick, s32[16]{0:T(128)S(1)} %copy-done.33, f32[16,3,128]{2,1,0:T(4,128)S(1)} %get-tuple-element.102.pos, ...), custom_call_target="tpu_custom_call" | custom-call | tf_op jit(solution)/shard_map/force/pallas_call | solution.py:441
  456.1 14.3 %omega.6 = f32[256,128]{1,0:T(8,128)S(1)} custom-call(s32[264]{0:T(512)S(1)} %get-tuple-element.85.list_c, s32[264]{0:T(512)S(1)} %copy-done.7, s32[264]{0:T(512)S(1)} %copy-done.22, s32[1]{0:T(128)} %get-tuple-element.87.number, f32[16,3,128]{2,1,0:T(4,128)S(1)} %get-tuple-element.117.pos, f32[17,128,128]{2,1,0:T(8,128)S(1)} %concatenate.6.widths, ...), custom_call_target="tpu_custom_call" | custom-call | tf_op jit(solution)/shard_map/omega/pallas_call | solution.py:449
  470.4 20.6 %all_to_all.278 = f32[32,8,128]{2,1,0:T(8,128)S(1)} all-to-all(f32[32,8,128]{2,1,0:T(8,128)S(1)} %bitcast.79), channel_id=1, replica_groups=mesh['gx'=4,'gy'=8] {'gx','gy'}, dimensions={0} | all-to-all | bytes 262144 | tf_op jit(solution)/shard_map/omega/all_to_all | solution.py:36
  491.0 9.9 %all_to_all.279 = f32[32,8,128]{2,1,0:T(8,128)S(1)} all-to-all(f32[32,8,128]{2,1,0:T(8,128)S(1)} %broadcast_in_dim.56), channel_id=1, replica_groups=mesh['gx'=4,'gy'=8] {'gx','gy'}, dimensions={0} | all-to-all | bytes 262144 | tf_op jit(solution)/shard_map/omega/all_to_all | solution.py:36
  500.9 0.7 copy-done.28
  501.6 30.3 %deposit.6 = (f32[16,128]{1,0:T(8,128)S(1)}, f32[16,3,128]{2,1,0:T(4,128)S(1)}, f32[16,128]{1,0:T(8,128)S(1)}, f32[16,16,128]{2,1,0:T(8,128)S(1)}, f32[256,128]{1,0:T(8,128)S(1)}, /*index=5*/f32[768,128]{1,0:T(8,128)S(1)}) custom-call(s32[264]{0:T(512)S(1)} %get-tuple-element.85.list_c, s32[264]{0:T(512)S(1)} %copy-done.7, s32[1]{0:T(128)} %get-tuple-element.87.number, ...), custom_call_target="tpu_custom_call" | custom-call | tf_op jit(solution)/shard_map/deposit/pallas_call | solution.py:458
  532.0 18.1 %all_to_all.280 = f32[32,8,128]{2,1,0:T(8,128)S(1)} all-to-all(f32[32,8,128]{2,1,0:T(8,128)S(1)} %bitcast.89), channel_id=1, replica_groups=mesh['gx'=4,'gy'=8] {'gx','gy'}, dimensions={0} | all-to-all | bytes 262144 | tf_op jit(solution)/shard_map/deposit/all_to_all | solution.py:36
  550.1 15.0 %all_to_all.281 = f32[32,24,128]{2,1,0:T(8,128)S(1)} all-to-all(f32[32,24,128]{2,1,0:T(8,128)S(1)} %bitcast.81), channel_id=1, replica_groups=mesh['gx'=4,'gy'=8] {'gx','gy'}, dimensions={0} | all-to-all | bytes 786432 | tf_op jit(solution)/shard_map/force/all_to_all | solution.py:36
  565.1 15.5 %all_to_all.282 = f32[32,24,128]{2,1,0:T(8,128)S(1)} all-to-all(f32[32,24,128]{2,1,0:T(8,128)S(1)} %bitcast.84), channel_id=1, replica_groups=mesh['gx'=4,'gy'=8] {'gx','gy'}, dimensions={0} | all-to-all | bytes 786432 | tf_op jit(solution)/shard_map/deposit/all_to_all | solution.py:36
  580.7 15.8 %density.7 = (f32[16,8,128]{2,1,0:T(8,128)S(1)}, f32[16,128]{1,0:T(8,128)S(1)}, f32[16,128]{1,0:T(8,128)S(1)}, f32[16,128]{1,0:T(8,128)S(1)}, f32[256,128]{1,0:T(8,128)S(1)}) custom-call(s32[128]{0:T(128)S(1)} %copy-done.19, s32[256]{0:T(256)S(1)} %get-tuple-element.75.pick, f32[16,3,128]{2,1,0:T(4,128)S(1)} %get-tuple-element.117.pos, ...), custom_call_target="tpu_custom_call" | custom-call | tf_op jit(solution)/shard_map/density/pallas_call | solution.py:434
  596.5 10.4 %all_to_all.283 = f32[32,8,128]{2,1,0:T(8,128)S(1)} all-to-all(f32[32,8,128]{2,1,0:T(8,128)S(1)} %bitcast.92), channel_id=1, replica_groups=mesh['gx'=4,'gy'=8] {'gx','gy'}, dimensions={0} | all-to-all | bytes 262144 | tf_op jit(solution)/shard_map/density/all_to_all | solution.py:36
  606.9 2.1 force.7
  609.0 14.3 %omega.7 = f32[256,128]{1,0:T(8,128)S(1)} custom-call(s32[264]{0:T(512)S(1)} %get-tuple-element.85.list_c, s32[264]{0:T(512)S(1)} %copy-done.7, s32[264]{0:T(512)S(1)} %copy-done.22, s32[1]{0:T(128)} %get-tuple-element.87.number, f32[16,3,128]{2,1,0:T(4,128)S(1)} %get-tuple-element.151.pos, f32[17,128,128]{2,1,0:T(8,128)S(1)} %concatenate.6.widths, ...), custom_call_target="tpu_custom_call" | custom-call | tf_op jit(solution)/shard_map/omega/pallas_call | solution.py:449
  623.3 22.4 %all_to_all.284 = f32[32,8,128]{2,1,0:T(8,128)S(1)} all-to-all(f32[32,8,128]{2,1,0:T(8,128)S(1)} %bitcast.76), channel_id=1, replica_groups=mesh['gx'=4,'gy'=8] {'gx','gy'}, dimensions={0} | all-to-all | bytes 262144 | tf_op jit(solution)/shard_map/omega/all_to_all | solution.py:36
  646.4 2.4 all-to-all-start.25
  649.4 7.8 %all-to-all-done.25 = f32[32,8,128]{2,1,0:T(8,128)S(1)} async-done(((f32[32,8,128]{2,1,0:T(8,128)}), f32[32,8,128]{2,1,0:T(8,128)S(1)}, u32[]{:S(2)}, u32[]{:S(2)}) %all-to-all-start.25) | async-done | bytes 131104 | tf_op jit(solution)/shard_map/omega/all_to_all | solution.py:36
  657.1 1.9 copy-done
  659.0 28.8 %deposit.7 = (f32[16,128]{1,0:T(8,128)}, f32[16,3,128]{2,1,0:T(4,128)S(1)}, f32[16,128]{1,0:T(8,128)}, f32[16,16,128]{2,1,0:T(8,128)}) custom-call(s32[264]{0:T(512)S(1)} %get-tuple-element.85.list_c, s32[264]{0:T(512)S(1)} %copy-done.7, s32[1]{0:T(128)} %get-tuple-element.87.number, s32[256]{0:T(256)S(1)} %get-tuple-element.75.pick, ...), custom_call_target="tpu_custom_call" | custom-call | tf_op jit(solution)/shard_map/deposit/pallas_call | solution.py:458
  (95 shorter events, 15.2 us)
Async XLA Ops:
  7.2 92.9 %copy-start.2 = (f32[16,128]{1,0:T(8,128)S(1)}, f32[16,128]{1,0:T(8,128)}, u32[]{:S(2)}) copy-start(f32[16,128]{1,0:T(8,128)} %smooth.17) | copy-start | bytes 24580
  7.2 92.9 %copy-start.9 = (f32[16,128]{1,0:T(8,128)S(1)}, f32[16,128]{1,0:T(8,128)}, u32[]{:S(2)}) copy-start(f32[16,128]{1,0:T(8,128)} %mass.5) | copy-start | bytes 24580
  7.2 92.9 %copy-start.13 = (f32[16,128]{1,0:T(8,128)S(1)}, f32[16,128]{1,0:T(8,128)}, u32[]{:S(2)}) copy-start(f32[16,128]{1,0:T(8,128)} %energy.3) | copy-start | bytes 24580
  7.2 142.1 %all-gather.2.cloned.1.call-start = ((), (), s32[]{:S(2)}) async-start(), calls=%async_computation.26 | async-start | bytes 4325376 | tf_op jit(solution)/shard_map/star_share/all_gather | solution.py:426
  20.3 111.1 %copy-start.18 = (s32[128]{0:T(128)}, s32[128]{0:T(128)S(1)}, u32[]{:S(2)}) copy-start(s32[128]{0:T(128)S(1)} %get-tuple-element.73.place) | copy-start | bytes 1540
  21.0 13.8 %all-to-all-start = ((s32[32,1,16]{2,1,0:T(1,128)}), s32[32,1,16]{2,1,0:T(1,128)S(1)}, u32[]{:S(2)}, u32[]{:S(2)}) async-start(s32[32,1,16]{2,1,0:T(1,128)} %bitcast), calls=%async_computation | async-start | bytes 32768 | tf_op jit(solution)/shard_map/plan/all_to_all | solution.py:36
  42.0 108.6 %copy-start.4 = (s32[264]{0:T(512)}, s32[264]{0:T(512)S(1)}, u32[]{:S(2)}) copy-start(s32[264]{0:T(512)S(1)} %get-tuple-element.86.list_slot) | copy-start | bytes 3172
  42.0 108.6 %copy-start.20 = (s32[264]{0:T(512)}, s32[264]{0:T(512)S(1)}, u32[]{:S(2)}) copy-start(s32[264]{0:T(512)S(1)} %get-tuple-element.88.list_out) | copy-start | bytes 3172
  42.0 0.7 copy-start.1
  42.7 0.7 copy-start.8
  57.2 74.2 %copy-start.31 = (s32[16]{0:T(128)S(1)}, s32[16]{0:T(128)}, u32[]{:S(2)}) copy-start(s32[16]{0:T(128)} %bins.7) | copy-start | bytes 196
  97.5 19.7 %all-to-all-start.4 = ((f32[32,8,128]{2,1,0:T(8,128)}), f32[32,8,128]{2,1,0:T(8,128)S(1)}, u32[]{:S(2)}, u32[]{:S(2)}) async-start(f32[32,8,128]{2,1,0:T(8,128)} %bitcast.7), calls=%async_computation.4 | async-start | bytes 262144 | tf_op jit(solution)/shard_map/start/all_to_all | solution.py:36
  116.6 0.6 copy-start.23
  117.2 14.2 %all-to-all-start.5 = ((f32[32,8,128]{2,1,0:T(8,128)}), f32[32,8,128]{2,1,0:T(8,128)S(1)}, u32[]{:S(2)}, u32[]{:S(2)}) async-start(f32[32,8,128]{2,1,0:T(8,128)} %bitcast.9), calls=%async_computation.5 | async-start | bytes 262144 | tf_op jit(solution)/shard_map/density/all_to_all | solution.py:36
  148.0 0.6 copy-start.11
  148.7 0.6 copy-start.25
  188.1 37.9 %all-to-all-start.8 = ((f32[32,24,128]{2,1,0:T(8,128)}), f32[32,24,128]{2,1,0:T(8,128)S(1)}, u32[]{:S(2)}, u32[]{:S(2)}) async-start(f32[32,24,128]{2,1,0:T(8,128)} %bitcast.17), calls=%async_computation.8 | async-start | bytes 786432 | tf_op jit(solution)/shard_map/force/all_to_all | solution.py:36
  190.5 3.9 copy-start.3
  190.5 3.9 copy-start.5
  190.5 3.9 copy-start.10
  190.5 3.9 copy-start.12
  190.5 3.9 copy-start.24
  190.6 3.9 copy-start.26
  224.8 0.6 copy-start.14
  225.4 0.6 copy-start.16
  247.5 93.9 %copy-start.7 = (s32[264]{0:T(512)S(1)}, s32[264]{0:T(512)}, u32[]{:S(2)}) copy-start(s32[264]{0:T(512)} %copy-done.4) | copy-start | bytes 3172
  262.7 0.7 copy-start.15
  263.4 0.7 copy-start.17
  264.1 0.7 copy-start.19
  290.8 0.7 copy-start.32
  292.9 0.6 copy-start.29
  293.5 0.7 copy-start.6
  294.1 0.7 copy-start.21
  341.4 0.7 copy-start.30
  342.1 105.3 %copy-start.33 = (s32[16]{0:T(128)S(1)}, s32[16]{0:T(128)}, u32[]{:S(2)}) copy-start(s32[16]{0:T(128)} %bins.7) | copy-start | bytes 196
  372.5 83.6 %copy-start.22 = (s32[264]{0:T(512)S(1)}, s32[264]{0:T(512)}, u32[]{:S(2)}) copy-start(s32[264]{0:T(512)} %copy-done.20) | copy-start | bytes 3172
  437.0 63.9 %copy-start.27 = (f32[16,128]{1,0:T(8,128)}, f32[16,128]{1,0:T(8,128)S(1)}, u32[]{:S(2)}) copy-start(f32[16,128]{1,0:T(8,128)S(1)} %get-tuple-element.121.density) | copy-start | bytes 24580
  500.9 0.7 copy-start.28
  501.6 105.3 %copy-start.34 = (s32[16]{0:T(128)S(1)}, s32[16]{0:T(128)}, u32[]{:S(2)}) copy-start(s32[16]{0:T(128)} %bins.7) | copy-start | bytes 196
  646.4 10.8 %all-to-all-start.25 = ((f32[32,8,128]{2,1,0:T(8,128)}), f32[32,8,128]{2,1,0:T(8,128)S(1)}, u32[]{:S(2)}, u32[]{:S(2)}) async-start(f32[32,8,128]{2,1,0:T(8,128)} %broadcast_in_dim.57), calls=%async_computation.25 | async-start | bytes 262144 | tf_op jit(solution)/shard_map/omega/all_to_all | solution.py:36
  657.1 1.9 copy-start
Sparse Core Ops, SparseCore 0:
  13.7 71.2 all-gather.1

commit v2 on v1

v2 whole, which is shorter than its diff:
```python
import jax
import jax.numpy as jnp
from jax import lax
from jax.experimental import pallas as pl
from jax.experimental.pallas import tpu as pltpu
from jax.sharding import PartitionSpec as P

SUBSTEPS = 4
KERNEL_NORM = 0.1795871221251666
GAMMA_LESS = 0.6666666666666666
TIME_STEP = 0.05
COOL_RATE = 0.4
ENERGY_FLOOR = 0.2
LOG2E = 1.4426950408889634
AXES = ("gx", "gy")
F32 = jnp.float32
BF16 = jnp.bfloat16
GROUP = 4
WIDE = 16
TEAM = 4
VMEM = pl.BlockSpec(memory_space=pltpu.VMEM)
SMEM = pl.BlockSpec(memory_space=pltpu.SMEM)
PARAMS = pltpu.CompilerParams(vmem_limit_bytes=48 * 1024 * 1024)


def call(body, outs, ins, scratch=(), smem_outs=(), work=0):
    return pl.pallas_call(
        body,
        out_shape=[jax.ShapeDtypeStruct(shape, dtype) for shape, dtype in outs],
        in_specs=ins,
        out_specs=[SMEM if at in smem_outs else VMEM for at in range(len(outs))],
        scratch_shapes=list(scratch),
        compiler_params=PARAMS,
        cost_estimate=pl.CostEstimate(flops=work, bytes_accessed=0, transcendentals=0) if work else None,
    )


def swap(payload):
    return lax.all_to_all(payload, AXES, split_axis=0, concat_axis=0, tiled=True)


def row_of(ref, at):
    return ref[pl.ds(at, 1), :]


def rows8(*rows):
    place = lax.broadcasted_iota(jnp.int32, (8, 128), 0)
    out = jnp.zeros((8, 128), F32)
    for at, row in enumerate(rows):
        out = jnp.where(place == at, row, out)
    return out


def split3(value):
    first = value.astype(BF16).astype(F32)
    rest = value - first
    second = rest.astype(BF16).astype(F32)
    third = (rest - second).astype(BF16).astype(F32)
    return first, second, third


def far_side(value):
    a, b, c = split3(value)
    return jnp.concatenate([a, a, b, b, a, c], axis=0).astype(BF16)


def near_side(value):
    a, b, c = split3(value)
    return jnp.concatenate([a, b, a, b, c, a], axis=0).T.astype(BF16)


def weights(value):
    a, b, c = split3(value)
    packed = jnp.concatenate([a, b, c, jnp.zeros_like(a)], axis=0).astype(BF16)
    return jnp.concatenate([packed, packed], axis=1)


def two_halves(value):
    first = value.astype(BF16)
    second = (value - first.astype(F32)).astype(BF16)
    return jnp.concatenate([first, second], axis=1)


def inner(left, right):
    return lax.dot_general(left, right, (((1,), (1,)), ((), ())), preferred_element_type=F32)


def outer(left, right):
    return lax.dot_general(left, right, (((1,), (0,)), ((), ())), preferred_element_type=F32)


def norm_sq(x, y, z):
    return x * x + y * y + z * z


def plan_kernel(peers, cap, sb):
    span = cap + sb

    def body(gas_dev, gas_slot, star_dev, star_slot, req, place, count):
        rows, neighbours = gas_dev.shape
        entries = star_dev.shape[1]

        def clear(d, _):
            count[d] = 0
            for c in range(span):
                req[d * span + c] = -1
            return 0

        def gas(b, _):
            for k in range(neighbours):
                dev = gas_dev[b, k]
                used = count[dev]
                count[dev] = used + 1
                req[dev * span + used] = gas_slot[b, k]
                place[b * neighbours + k] = dev * cap + used
            return 0

        def star(c, _):
            for at in range(entries):
                req[star_dev[c, at] * span + cap + c] = star_slot[c, at]
            return 0

        lax.fori_loop(0, peers, clear, 0)
        lax.fori_loop(0, rows, gas, 0)
        lax.fori_loop(0, sb, star, 0)

    return body


def list_sizes(stars, nb):
    room = stars + nb * GROUP + WIDE
    room = -(-room // WIDE) * WIDE
    return room, room + stars


def list_kernel(peers, cap, sb, nb):
    span = cap + sb
    room, whole = list_sizes(peers * sb, nb)

    def body(asked, list_c, list_slot, number, count):
        for b in range(nb + 1):
            count[b] = 0

        def clear(at, _):
            for g in range(GROUP):
                list_c[at * GROUP + g] = -1
            list_slot[at] = nb
            return 0

        lax.fori_loop(0, room // GROUP, clear, 0, unroll=2)

        def tally(d, _):
            for c in range(sb):
                slot = asked[d * span + cap + c] + 1
                count[slot] = count[slot] + 1
            return 0

        lax.fori_loop(0, peers, tally, 0)
        count[0] = room
        used = 0
        for b in range(nb):
            more = (count[b + 1] + GROUP - 1) // GROUP * GROUP
            count[b + 1] = used
            used = used + more
        number[0] = (used + WIDE - 1) // WIDE

        def deal(d, _):
            for c in range(sb):
                slot = asked[d * span + cap + c]
                at = count[slot + 1]
                count[slot + 1] = at + 1
                list_c[at] = d * sb + c
                list_slot[at // GROUP] = slot
            return 0

        lax.fori_loop(0, peers, deal, 0)

    return body


def send_rows(asked, out, source, width, cap, span):
    def one(d, _):
        for c in range(cap):
            slot = jnp.maximum(asked[d * span + c], 0)
            for f in range(width):
                out[pl.ds((d * cap + c) * width + f, 1), :] = source(slot, f)
        return 0

    lax.fori_loop(0, out.shape[0] // (cap * width), one, 0)


def start_kernel(cap, span):
    def body(asked, pos, vel, mass, smooth, send, widths):
        def source(slot, f):
            if f < 3:
                return pos[slot, f : f + 1, :]
            if f >= 5:
                return vel[slot, f - 5 : f - 4, :]
            return row_of(smooth if f == 3 else mass, slot)

        send_rows(asked, send, source, 8, cap, span)
        blocks = pos.shape[0]

        def one(b, _):
            h = row_of(smooth, b)
            widths[b] = jnp.broadcast_to(h * h, widths.shape[1:]).T
            return 0

        lax.fori_loop(0, blocks, one, 0, unroll=2)
        widths[blocks] = jnp.ones(widths.shape[1:], F32)

    return body


def share_kernel(star_pos, star_vel, star_radius, star_mdot, star_edot, star_yields, share):
    for c in range(star_pos.shape[0]):
        radius = star_radius[c : c + 1, :]
        ejecta = star_mdot[c : c + 1, :] * TIME_STEP
        share[c, 0:3, :] = star_pos[c]
        share[c, 3:6, :] = star_vel[c]
        share[c, 6:7, :] = -LOG2E / (radius * radius)
        share[c, 7:8, :] = jnp.zeros_like(ejecta)
        share[c, 8:9, :] = ejecta
        share[c, 9:12, :] = ejecta * star_vel[c]
        share[c, 12:13, :] = star_edot[c : c + 1, :] * TIME_STEP
        share[c, 13:16, :] = jnp.zeros_like(star_vel[c])
        share[c, 16:32, :] = ejecta * star_yields[c]


def total_kernel(peers):
    def body(parts, total):
        sb = total.shape[0] // peers
        now = parts[0:sb, :]
        for d in range(1, peers):
            now = now + parts[d * sb : (d + 1) * sb, :]
        for d in range(peers):
            total[d * sb : (d + 1) * sb, :] = now

    return body


def team_sums(jobs):
    exponents = [[outer(near, far) for near, far, _ in team] for team in jobs]
    reaches = [[two_halves(jnp.exp2(one)) for one in team] for team in exponents]
    results = []
    for team, parts in zip(jobs, reaches):
        total = None
        for (_, _, load), part in zip(team, parts):
            one = inner(part, load)
            total = one if total is None else total + one
        total = total.T
        results.append(total[0:8] + total[8:16] + total[16:24])
    return results


def density_kernel(neighbours, cap, span, first):
    def body(asked, place, pos, vel, mass, smooth, energy, *rest):
        if first:
            far0, sums, term, gain, density, send_gain = rest
        else:
            far_pos, far_mv, sums, term, gain, density, send_gain = rest

        def ghost(at):
            if first:
                return [row_of(far0, at * 8 + f) for f in (0, 1, 2, 5, 6, 7, 4)]
            return [row_of(far_pos, at * 3 + f) for f in range(3)] + [row_of(far_mv, at * 4 + f) for f in (1, 2, 3, 0)]

        def pair(near, px, py, pz, vx, vy, vz, m):
            far = far_side(rows8(px, py, pz, norm_sq(px, py, pz), 1.0))
            load = rows8(m, m * px, m * py, m * pz, m * vx, m * vy, m * vz, m * (px * vx + py * vy + pz * vz))
            return near, far, weights(load)

        def team(at, _):
            jobs = []
            for g in range(TEAM):
                b = at * TEAM + g
                x, y, z = (pos[b, f : f + 1, :] for f in range(3))
                h = row_of(smooth, b)
                scale = LOG2E / (h * h)
                near = near_side(
                    rows8(2.0 * scale * x, 2.0 * scale * y, 2.0 * scale * z, -scale, -scale * norm_sq(x, y, z))
                )
                own = [pair(near, x, y, z, *(vel[b, f : f + 1, :] for f in range(3)), row_of(mass, b))]
                jobs.append(own + [pair(near, *ghost(place[b * neighbours + k])) for k in range(neighbours)])
            for g, total in enumerate(team_sums(jobs)):
                b = at * TEAM + g
                h = row_of(smooth, b)
                sums[b] = total
                dense = KERNEL_NORM * total[0:1] / (h * h * h)
                density[pl.ds(b, 1), :] = dense
                own = GAMMA_LESS * row_of(energy, b) / dense
                term[pl.ds(b, 1), :] = own
                gain[pl.ds(b, 1), :] = row_of(mass, b) * own * ((2.0 * KERNEL_NORM) / (h * h * h * h * h))
            return 0

        lax.fori_loop(0, pos.shape[0] // TEAM, team, 0)
        send_rows(asked, send_gain, lambda slot, f: row_of(gain, slot), 1, cap, span)

    return body


def force_kernel(neighbours, cap, span, substep, first, last):
    def body(asked, place, bins, pos, vel, smooth, energy, term, gain, sums, far0, *rest):
        if first:
            far_gain, new_pos, new_vel, new_energy = rest[:4]
        else:
            far_pos, far_gain, new_pos, new_vel, new_energy = rest[:5]
        busy = rest[-1]

        def ghost(at):
            if first:
                return [row_of(far0, at * 8 + f) for f in range(4)] + [row_of(far_gain, at)]
            return [row_of(far_pos, at * 3 + f) for f in range(3)] + [row_of(far0, at * 8 + 3), row_of(far_gain, at)]

        def pair(near, px, py, pz, width, push):
            scale = LOG2E / (width * width)
            far = far_side(rows8(scale * px, scale * py, scale * pz, scale * norm_sq(px, py, pz), scale))
            return near, far, weights(rows8(push, push * px, push * py, push * pz))

        new_energy[...] = energy[...]
        used = 0
        for b in range(pos.shape[0]):
            new_vel[b] = vel[b]
            new_pos[b] = pos[b] + TIME_STEP * vel[b]
            period = jnp.left_shift(1, bins[b])
            busy[used] = b
            used = used + jnp.where((substep & (period - 1)) == 0, 1, 0)
        edge = busy[jnp.maximum(used - 1, 0)]
        for extra in range(TEAM):
            busy[used + extra] = edge

        def team(at, _):
            jobs = []
            for g in range(TEAM):
                b = busy[at * TEAM + g]
                x, y, z = (pos[b, f : f + 1, :] for f in range(3))
                near = near_side(rows8(2.0 * x, 2.0 * y, 2.0 * z, -1.0, -norm_sq(x, y, z)))
                own = [pair(near, x, y, z, row_of(smooth, b), row_of(gain, b))]
                jobs.append(own + [pair(near, *ghost(place[b * neighbours + k])) for k in range(neighbours)])
            for g, total in enumerate(team_sums(jobs)):
                b = busy[at * TEAM + g]
                x, y, z = (pos[b, f : f + 1, :] for f in range(3))
                u, v, w = (vel[b, f : f + 1, :] for f in range(3))
                h = row_of(smooth, b)
                near_sum = sums[b]
                grad = row_of(term, b) * ((2.0 * KERNEL_NORM) / (h * h * h * h * h))
                kick = TIME_STEP * jnp.left_shift(1, bins[b]).astype(F32)
                heat = (
                    (x * u + y * v + z * w) * near_sum[0:1]
                    - (u * near_sum[1:2] + v * near_sum[2:3] + w * near_sum[3:4])
                    - (x * near_sum[4:5] + y * near_sum[5:6] + z * near_sum[6:7])
                    + near_sum[7:8]
                )
                new_energy[pl.ds(b, 1), :] = row_of(energy, b) - kick * (grad * heat)
                for f, (speed, spot) in enumerate(((u, x), (v, y), (w, z))):
                    one = grad * (spot * near_sum[0:1] - near_sum[f + 1 : f + 2])
                    two = spot * total[0:1] - total[f + 1 : f + 2]
                    now = speed + kick * (one + two)
                    new_vel[b, f : f + 1, :] = now
                    new_pos[b, f : f + 1, :] = spot + TIME_STEP * now
            return 0

        lax.fori_loop(0, (used + TEAM - 1) // TEAM, team, 0)
        if not last:
            send_rows(asked, rest[-2], lambda slot, f: new_pos[slot, f : f + 1, :], 3, cap, span)

    return body


def gas_sides(pos, sides):
    def one(b, _):
        x, y, z = (pos[b, f : f + 1, :] for f in range(3))
        sides[b] = near_side(rows8(-2.0 * x, -2.0 * y, -2.0 * z, 1.0, norm_sq(x, y, z)))
        return 0

    blocks = pos.shape[0]
    lax.fori_loop(0, blocks, one, 0, unroll=4)
    sides[blocks] = jnp.zeros(sides.shape[1:], BF16)


def omegas(list_c, list_slot, at, when, star, sides, widths):
    entries = []
    for e in range(WIDE):
        entries.append((list_c[at * WIDE + e], list_slot[at * (WIDE // GROUP) + e // GROUP]))
    dist = []
    for c, slot in entries:
        c = jnp.maximum(c, 0)
        x, y, z = (star[c, f : f + 1, :] + when * star[c, f + 3 : f + 4, :] for f in range(3))
        dist.append(outer(sides[slot], far_side(rows8(x, y, z, norm_sq(x, y, z), 1.0))))
    out = []
    for (c, slot), one in zip(entries, dist):
        one = jnp.maximum(one, 1e-30)
        wide = one + widths[slot]
        reach = star[jnp.maximum(c, 0), 6:7, :]
        out.append((c, slot, (1.0 - one * lax.rsqrt(one * wide)) * jnp.exp2(one * reach)))
    return out


def omega_kernel(substep):
    when = (substep + 1) * TIME_STEP

    def body(list_c, list_slot, number, pos, widths, star, part, sides, room):
        gas_sides(pos, sides)
        room[...] = jnp.zeros_like(room)
        trash = part.shape[0]

        def group(at, _):
            for c, _, omega in omegas(list_c, list_slot, at, when, star, sides, widths):
                room[pl.ds(jnp.where(c < 0, trash, c), 1), :] = jnp.sum(omega, axis=0, keepdims=True)
            return 0

        lax.fori_loop(0, number[0], group, 0)
        part[...] = room[0 : part.shape[0], :]

    return body


def deposit_kernel(substep, last, cap, span):
    when = (substep + 1) * TIME_STEP

    def body(
        asked, list_c, list_slot, number, pos, widths, star, pay, total, mass, vel, energy, metals, density, *rest
    ):
        new_mass, new_vel, new_energy, new_metals = rest[:4]
        sides, dep = rest[-2:]
        gas_sides(pos, sides)
        dep[...] = jnp.zeros_like(dep)

        def group(at, _):
            found = omegas(list_c, list_slot, at, when, star, sides, widths)
            rights = [two_halves(omega) for _, _, omega in found]
            lefts = []
            for c, _, _ in found:
                flag = jnp.where(c < 0, 0.0, 1.0)
                c = jnp.maximum(c, 0)
                load = pay[c] * (flag / row_of(total, c))
                first = load.astype(BF16).astype(F32)
                left = jnp.concatenate([first, load - first], axis=0).astype(BF16)
                lefts.append(jnp.concatenate([left, left], axis=1))
            for g in range(0, WIDE, GROUP):
                out = None
                for right, left in zip(rights[g : g + GROUP], lefts[g : g + GROUP]):
                    one = inner(right, left)
                    out = one if out is None else out + one
                slot = found[g][1]
                dep[slot] = dep[slot] + out
            return 0

        lax.fori_loop(0, number[0], group, 0)

        def block(b, _):
            got = dep[b].T
            got = got[0:24] + got[24:48]
            m = row_of(mass, b)
            grown = m + got[0:1]
            new_mass[pl.ds(b, 1), :] = grown
            new_vel[b] = (m * vel[b] + got[1:4]) / grown
            cooled = ENERGY_FLOOR + (row_of(energy, b) - ENERGY_FLOOR) * jnp.exp(
                (-TIME_STEP * COOL_RATE) * row_of(density, b)
            )
            new_energy[pl.ds(b, 1), :] = (m * cooled + got[4:5]) / grown
            new_metals[b] = metals[b] + got[8:24]
            return 0

        lax.fori_loop(0, pos.shape[0], block, 0, unroll=4)
        if not last:
            send_rows(
                asked,
                rest[4],
                lambda slot, f: new_vel[slot, f - 1 : f, :] if f else row_of(new_mass, slot),
                4,
                cap,
                span,
            )

    return body


def local(
    gas_pos, gas_vel, gas_mass, gas_smooth, gas_energy, gas_metals, gas_bins, gas_nbr_dev, gas_nbr_slot,
    star_pos, star_vel, star_radius, star_mdot, star_edot, star_yields, star_ovl_dev, star_ovl_slot,
):
    peers = lax.axis_size(AXES)
    nb, neighbours = gas_nbr_dev.shape
    sb = star_ovl_dev.shape[0]
    width = gas_pos.shape[2]
    cap = max(2, 2 * nb * neighbours // peers)
    span = cap + sb
    stars = peers * sb
    sent = peers * cap
    i32 = jnp.int32
    room, whole = list_sizes(stars, nb)
    heavy = 10**10

    with jax.named_scope("plan"):
        req, place = call(
            plan_kernel(peers, cap, sb),
            [((peers * span,), i32), ((nb * neighbours,), i32)],
            [SMEM] * 4,
            [pltpu.SMEM((peers,), i32)],
            smem_outs=(0, 1),
        )(gas_nbr_dev, gas_nbr_slot, star_ovl_dev, star_ovl_slot)
        asked = swap(req.reshape(peers, span)).reshape(-1)

    with jax.named_scope("share"):
        share = call(share_kernel, [((sb, 32, width), F32)], [VMEM] * 6)(
            star_pos, star_vel, star_radius, star_mdot, star_edot, star_yields
        )[0]
        all_stars = lax.all_gather(share, AXES, axis=0, tiled=True)
        all_star8, all_pay = all_stars[:, 0:8], all_stars[:, 8:32]

    with jax.named_scope("start"):
        send0, widths = call(
            start_kernel(cap, span),
            [((sent * 8, width), F32), ((nb + 1, width, width), F32)],
            [SMEM] + [VMEM] * 4,
        )(asked, gas_pos, gas_vel, gas_mass, gas_smooth)
        far0 = swap(send0)
        list_c, list_slot, number = call(
            list_kernel(peers, cap, sb, nb),
            [((whole,), i32), ((whole // GROUP,), i32), ((1,), i32)],
            [SMEM],
            [pltpu.SMEM((nb + 1,), i32)],
            smem_outs=range(3),
        )(asked)

    pos, vel, mass, energy, metals = gas_pos, gas_vel, gas_mass, gas_energy, gas_metals
    sides = pltpu.VMEM((nb + 1, width, 48), BF16)
    block3, block1 = ((nb, 3, width), F32), ((nb, width), F32)
    for substep in range(SUBSTEPS):
        first, last = substep == 0, substep == SUBSTEPS - 1
        with jax.named_scope("density"):
            far = [far0] if first else [far_pos, far_mv]
            sums, term, gain, density, send_gain = call(
                density_kernel(neighbours, cap, span, first),
                [((nb, 8, width), F32), block1, block1, block1, ((sent, width), F32)],
                [SMEM] * 2 + [VMEM] * (5 + len(far)),
                work=heavy,
            )(asked, place, pos, vel, mass, gas_smooth, energy, *far)
            far_gain = swap(send_gain)
        with jax.named_scope("force"):
            far = [far0] if first else [far0, far_pos]
            outs = call(
                force_kernel(neighbours, cap, span, substep, first, last),
                [block3, block3, block1] + ([] if last else [((sent * 3, width), F32)]),
                [SMEM] * 3 + [VMEM] * (8 + len(far)),
                [pltpu.SMEM((nb + TEAM,), i32)],
                work=heavy,
            )(asked, place, gas_bins, pos, vel, gas_smooth, energy, term, gain, sums, *far, far_gain)
            pos, vel, energy = outs[:3]
            if not last:
                far_pos = swap(outs[3])
        with jax.named_scope("omega"):
            part = call(
                omega_kernel(substep),
                [((stars, width), F32)],
                [SMEM] * 3 + [VMEM] * 3,
                [sides, pltpu.VMEM((stars + 8, width), F32)],
                work=heavy,
            )(list_c, list_slot, number, pos, widths, all_star8)[0]
            if not last:
                part, far_pos = lax.optimization_barrier((part, far_pos))
            total = swap(call(total_kernel(peers), [((stars, width), F32)], [VMEM])(swap(part))[0])
        with jax.named_scope("deposit"):
            outs = call(
                deposit_kernel(substep, last, cap, span),
                [block1, block3, block1, ((nb, 16, width), F32)] + ([] if last else [((sent * 4, width), F32)]),
                [SMEM] * 4 + [VMEM] * 10,
                [sides, pltpu.VMEM((nb + 1, width, 48), F32)],
                work=heavy,
            )(asked, list_c, list_slot, number, pos, widths, all_star8, all_pay, total, mass, vel, energy, metals, density)
            mass, vel, energy, metals = outs[:4]
            if not last:
                far_mv = swap(outs[4])
    return (pos, vel, mass, energy, metals)


def solution(mesh):
    split = [P(AXES, *([None] * (rank - 1))) for rank in (3, 3, 2, 2, 2, 3, 1, 2, 2, 3, 3, 2, 2, 2, 3, 2, 2)]
    return jax.shard_map(
        local,
        mesh=mesh,
        in_specs=tuple(split),
        out_specs=tuple(P(AXES, *([None] * (rank - 1))) for rank in (3, 3, 2, 2, 3)),
        check_vma=False,
    )
```

time: 707 us -> 451 us (0.64)
  Pallas kernels: 282 us -> 104 us
  blocking collectives: 325 us -> 223 us
  waiting for transfers between devices: 20.8 us -> 40.8 us
  starting transfers between devices: 20.4 us -> 30.2 us
    pallas_call x19 -> x24, Pallas kernels: 282 us -> 104 us  [the longest x4 34.4 us: local(): call(deposit_kernel(substep, last, cap, span), [block1, block3, block1, (...]
    all_to_all x21 -> x13, blocking collectives: 325 us -> 223 us  [swap(): lax.all_to_all(payload, AXES, split_axis=0, concat_axis=0, tiled=True)]
    all_to_all x5 -> x7, waiting for transfers between devices: 20.7 us -> 40.8 us  [swap(): lax.all_to_all(payload, AXES, split_axis=0, concat_axis=0, tiled=True)]
    all_to_all x5 -> x7, starting transfers between devices: 20.4 us -> 30.1 us  [swap(): lax.all_to_all(payload, AXES, split_axis=0, concat_axis=0, tiled=True)]
    unnamed x77 -> x66, local copies, waits for them, and re-layouts: 17.4 us -> 24.7 us
  transfers between devices with their start and end apart: 6 -> 8, of which waited for: 3 -> 7; matrix products, arithmetic and copies ran while one was open for 2% -> 2% of each run, Pallas kernels for 11% -> 9%
where the time goes in v2:
time: 451 us; the launch traced here: 444 us
  blocking collectives  223 us (49%)
  Pallas kernels  104 us (23%)
  waiting for transfers between devices  40.8 us (9%)
  local copies, waits for them, and re-layouts  31.1 us (7%)
  starting transfers between devices  30.2 us (7%)
  between operations  14.3 us (3%)
    all_to_all x13, blocking collectives, swap(): lax.all_to_all(payload, AXES, split_axis=0, concat_axis=0, tiled=True)  223 us
    all_to_all x7, waiting for transfers between devices, swap(): lax.all_to_all(payload, AXES, split_axis=0, concat_axis=0, tiled=True)  40.8 us
    pallas_call x4, Pallas kernels, local(): call(deposit_kernel(substep, last, cap, span), [block1, block3, block1, (...  34.4 us
    all_to_all x7, starting transfers between devices, swap(): lax.all_to_all(payload, AXES, split_axis=0, concat_axis=0, tiled=True)  30.1 us
    pallas_call x4, Pallas kernels, local(): call(density_kernel(neighbours, cap, span, first), [((nb, 8, width), F32)...  25.2 us
    unnamed x66, local copies, waits for them, and re-layouts  24.7 us
    pallas_call x4, Pallas kernels, local(): call(omega_kernel(substep), [((stars, width), F32)], [SMEM] * 3 + [VMEM]...  19.6 us
    pallas_call x4, Pallas kernels, local(): call(force_kernel(neighbours, cap, span, substep, first, last), [block3,...  11.8 us
  transfers between devices with their start and end apart: 8, of which 7 were waited for; matrix products, arithmetic and copies ran while one was open for 2% of the time, Pallas kernels for 9%

profile of v2, /device:TPU:1, one launch (start us, length us, event | category | flops | bytes accessed | tf_op | source)
XLA Modules:
  0.0 444.1 jit_solution(7821209416878306882)
XLA Ops:
  7.2 0.7 copy.55.star_pos
  7.9 0.7 copy.56.star_vel
  8.6 0.8 copy-done.4
  11.5 0.7 share.1
  12.3 0.8 copy.46.gas_dev
  13.0 0.8 copy.47.gas_slot
  15.2 3.1 plan.1
  19.0 7.1 %all-to-all-start = ((s32[32,1,16]{2,1,0:T(1,128)}), s32[32,1,16]{2,1,0:T(1,128)S(1)}, u32[]{:S(2)}, u32[]{:S(2)}) async-start(s32[32,1,16]{2,1,0:T(1,128)} %bitcast), calls=%async_computation | async-start | bytes 32768 | tf_op jit(solution)/shard_map/plan/all_to_all | solution.py:39
  26.1 0.8 copy.53.pos
  26.8 0.8 copy.54.vel
  27.6 5.2 %all-to-all-done = s32[32,1,16]{2,1,0:T(1,128)S(1)} async-done(((s32[32,1,16]{2,1,0:T(1,128)}), s32[32,1,16]{2,1,0:T(1,128)S(1)}, u32[]{:S(2)}, u32[]{:S(2)}) %all-to-all-start) | async-done | bytes 2080 | tf_op jit(solution)/shard_map/plan/all_to_all | solution.py:39
  34.1 0.7 copy-done.5
  35.5 2.4 start.2
  37.8 40.0 %all_to_all.221 = f32[32,64,128]{2,1,0:T(8,128)S(1)} all-to-all(f32[32,64,128]{2,1,0:T(8,128)S(1)} %bitcast.44), channel_id=1, replica_groups=mesh['gx'=4,'gy'=8] {'gx','gy'}, dimensions={0} | all-to-all | bytes 2097152 | tf_op jit(solution)/shard_map/start/all_to_all | solution.py:39
  79.9 6.8 %density.4 = (f32[16,8,128]{2,1,0:T(8,128)S(1)}, f32[16,128]{1,0:T(8,128)S(1)}, f32[16,128]{1,0:T(8,128)S(1)}, f32[16,128]{1,0:T(8,128)S(1)}, f32[256,128]{1,0:T(8,128)}) custom-call(s32[512]{0:T(512)S(1)} %reshape.56.asked, s32[128]{0:T(128)S(1)} %get-tuple-element.73.place, f32[16,3,128]{2,1,0:T(4,128)S(1)} %copy.53.pos, f32[16,3,128]{2,1,0:T(4,128)S(1)} %copy.54.vel, ...), custom_call_target="tpu_custom_call" | custom-call | flops 10000000000 | tf_op jit(solution)/shard_map/density/pallas_call | solution.py:534
  86.7 3.4 all-to-all-start.2
  90.2 5.3 %start.3 = (s32[592]{0:T(1024)S(1)}, s32[148]{0:T(256)S(1)}, s32[1]{0:T(128)}) custom-call(s32[512]{0:T(512)S(1)} %reshape.56.asked), custom_call_target="tpu_custom_call" | custom-call | tf_op jit(solution)/shard_map/start/pallas_call | solution.py:519
  95.4 3.1 all-to-all-done.2
  98.5 7.1 %force.4 = (f32[16,3,128]{2,1,0:T(4,128)S(1)}, f32[16,3,128]{2,1,0:T(4,128)S(1)}, f32[16,128]{1,0:T(8,128)S(1)}, f32[768,128]{1,0:T(8,128)}) custom-call(s32[512]{0:T(512)S(1)} %reshape.56.asked, s32[128]{0:T(128)S(1)} %get-tuple-element.73.place, s32[16]{0:T(128)S(1)} %copy-done.28, f32[16,3,128]{2,1,0:T(4,128)S(1)} %copy.53.pos, ...), custom_call_target="tpu_custom_call" | custom-call | flops 10000000000 | tf_op jit(solution)/shard_map/force/pallas_call | solution.py:543
  105.7 2.9 all-to-all-start.3
  108.6 1.3 slice.8.star
  109.9 1.6 copy-done.17
  111.5 4.9 %omega.8 = f32[256,128]{1,0:T(8,128)S(1)} custom-call(s32[592]{0:T(1024)S(1)} %get-tuple-element.80.list_c, s32[148]{0:T(256)S(1)} %get-tuple-element.81.list_slot, s32[1]{0:T(128)} %get-tuple-element.82.number, f32[16,3,128]{2,1,0:T(4,128)S(1)} %get-tuple-element.79.pos, f32[17,128,128]{2,1,0:T(8,128)S(1)} %copy-done.17, f32[256,8,128]{2,1,0:T(8,128)S(1)} %slice.8.star), custom_call_target="tpu_custom_call" | custom-call | flops 10000000000 | tf_op jit(solution)/shard_map/omega/pallas_call | solution.py:554
  116.4 5.6 %all-to-all-done.3 = f32[32,24,128]{2,1,0:T(8,128)S(1)} async-done(((f32[32,24,128]{2,1,0:T(8,128)}), f32[32,24,128]{2,1,0:T(8,128)S(1)}, u32[]{:S(2)}, u32[]{:S(2)}) %all-to-all-start.3) | async-done | bytes 393248 | tf_op jit(solution)/shard_map/force/all_to_all | solution.py:39
  122.0 13.1 %all_to_all.222 = f32[32,8,128]{2,1,0:T(8,128)S(1)} all-to-all(f32[32,8,128]{2,1,0:T(8,128)S(1)} %bitcast.74), channel_id=1, replica_groups=mesh['gx'=4,'gy'=8] {'gx','gy'}, dimensions={0} | all-to-all | bytes 262144 | tf_op jit(solution)/shard_map/omega/all_to_all | solution.py:39
  135.8 2.4 all-to-all-start.5
  138.2 3.8 slice.9.pay
  142.0 4.5 %all-to-all-done.5 = f32[32,8,128]{2,1,0:T(8,128)S(1)} async-done(((f32[32,8,128]{2,1,0:T(8,128)}), f32[32,8,128]{2,1,0:T(8,128)S(1)}, u32[]{:S(2)}, u32[]{:S(2)}) %all-to-all-start.5) | async-done | bytes 131104 | tf_op jit(solution)/shard_map/omega/all_to_all | solution.py:39
  146.6 1.2 copy-done.18
  147.8 8.9 %deposit.4 = (f32[16,128]{1,0:T(8,128)S(1)}, f32[16,3,128]{2,1,0:T(4,128)S(1)}, f32[16,128]{1,0:T(8,128)S(1)}, f32[16,16,128]{2,1,0:T(8,128)S(1)}, f32[1024,128]{1,0:T(8,128)S(1)}) custom-call(s32[512]{0:T(512)S(1)} %reshape.56.asked, s32[592]{0:T(1024)S(1)} %get-tuple-element.80.list_c, s32[148]{0:T(256)S(1)} %get-tuple-element.81.list_slot, ...), custom_call_target="tpu_custom_call" | custom-call | flops 10000000000 | tf_op jit(solution)/shard_map/deposit/pallas_call | solution.py:565
  156.7 26.3 %all_to_all.223 = f32[32,32,128]{2,1,0:T(8,128)S(1)} all-to-all(f32[32,32,128]{2,1,0:T(8,128)S(1)} %bitcast.47), channel_id=1, replica_groups=mesh['gx'=4,'gy'=8] {'gx','gy'}, dimensions={0} | all-to-all | bytes 1048576 | tf_op jit(solution)/shard_map/deposit/all_to_all | solution.py:39
  183.0 6.1 %density.5 = (f32[16,8,128]{2,1,0:T(8,128)S(1)}, f32[16,128]{1,0:T(8,128)S(1)}, f32[16,128]{1,0:T(8,128)S(1)}, f32[16,128]{1,0:T(8,128)S(1)}, f32[256,128]{1,0:T(8,128)S(1)}) custom-call(s32[512]{0:T(512)S(1)} %reshape.56.asked, s32[128]{0:T(128)S(1)} %get-tuple-element.73.place, f32[16,3,128]{2,1,0:T(4,128)S(1)} %get-tuple-element.79.pos, ...), custom_call_target="tpu_custom_call" | custom-call | flops 10000000000 | tf_op jit(solution)/shard_map/density/pallas_call | solution.py:534
  189.1 10.5 %all_to_all.224 = f32[32,8,128]{2,1,0:T(8,128)S(1)} all-to-all(f32[32,8,128]{2,1,0:T(8,128)S(1)} %bitcast.71), channel_id=1, replica_groups=mesh['gx'=4,'gy'=8] {'gx','gy'}, dimensions={0} | all-to-all | bytes 262144 | tf_op jit(solution)/shard_map/density/all_to_all | solution.py:39
  199.6 2.0 force.5
  201.7 5.0 %all-to-all-start.8 = ((f32[32,24,128]{2,1,0:T(8,128)}), f32[32,24,128]{2,1,0:T(8,128)S(1)}, u32[]{:S(2)}, u32[]{:S(2)}) async-start(f32[32,24,128]{2,1,0:T(8,128)} %bitcast.15), calls=%async_computation.8 | async-start | bytes 786432 | tf_op jit(solution)/shard_map/force/all_to_all | solution.py:39
  206.7 1.2 copy-done.19
  208.0 4.8 %omega.10 = f32[256,128]{1,0:T(8,128)S(1)} custom-call(s32[592]{0:T(1024)S(1)} %get-tuple-element.80.list_c, s32[148]{0:T(256)S(1)} %get-tuple-element.81.list_slot, s32[1]{0:T(128)} %get-tuple-element.82.number, f32[16,3,128]{2,1,0:T(4,128)S(1)} %get-tuple-element.98.pos, f32[17,128,128]{2,1,0:T(8,128)S(1)} %copy-done.19, f32[256,8,128]{2,1,0:T(8,128)S(1)} %slice.8.star), custom_call_target="tpu_custom_call" | custom-call | flops 10000000000 | tf_op jit(solution)/shard_map/omega/pallas_call | solution.py:554
  212.8 7.3 %all-to-all-done.8 = f32[32,24,128]{2,1,0:T(8,128)S(1)} async-done(((f32[32,24,128]{2,1,0:T(8,128)}), f32[32,24,128]{2,1,0:T(8,128)S(1)}, u32[]{:S(2)}, u32[]{:S(2)}) %all-to-all-start.8) | async-done | bytes 393248 | tf_op jit(solution)/shard_map/force/all_to_all | solution.py:39
  220.1 11.4 %all_to_all.225 = f32[32,8,128]{2,1,0:T(8,128)S(1)} all-to-all(f32[32,8,128]{2,1,0:T(8,128)S(1)} %bitcast.75), channel_id=1, replica_groups=mesh['gx'=4,'gy'=8] {'gx','gy'}, dimensions={0} | all-to-all | bytes 262144 | tf_op jit(solution)/shard_map/omega/all_to_all | solution.py:39
  231.6 9.9 %all_to_all.226 = f32[32,8,128]{2,1,0:T(8,128)S(1)} all-to-all(f32[32,8,128]{2,1,0:T(8,128)S(1)} %bitcast.53), channel_id=1, replica_groups=mesh['gx'=4,'gy'=8] {'gx','gy'}, dimensions={0} | all-to-all | bytes 262144 | tf_op jit(solution)/shard_map/omega/all_to_all | solution.py:39
  241.5 1.2 copy-done.20
  242.7 8.9 %deposit.5 = (f32[16,128]{1,0:T(8,128)S(1)}, f32[16,3,128]{2,1,0:T(4,128)S(1)}, f32[16,128]{1,0:T(8,128)S(1)}, f32[16,16,128]{2,1,0:T(8,128)S(1)}, f32[1024,128]{1,0:T(8,128)S(1)}) custom-call(s32[512]{0:T(512)S(1)} %reshape.56.asked, s32[592]{0:T(1024)S(1)} %get-tuple-element.80.list_c, s32[148]{0:T(256)S(1)} %get-tuple-element.81.list_slot, ...), custom_call_target="tpu_custom_call" | custom-call | flops 10000000000 | tf_op jit(solution)/shard_map/deposit/pallas_call | solution.py:565
  251.7 26.3 %all_to_all.227 = f32[32,32,128]{2,1,0:T(8,128)S(1)} all-to-all(f32[32,32,128]{2,1,0:T(8,128)S(1)} %bitcast.45), channel_id=1, replica_groups=mesh['gx'=4,'gy'=8] {'gx','gy'}, dimensions={0} | all-to-all | bytes 1048576 | tf_op jit(solution)/shard_map/deposit/all_to_all | solution.py:39
  278.0 6.1 %density.6 = (f32[16,8,128]{2,1,0:T(8,128)S(1)}, f32[16,128]{1,0:T(8,128)S(1)}, f32[16,128]{1,0:T(8,128)S(1)}, f32[16,128]{1,0:T(8,128)S(1)}, f32[256,128]{1,0:T(8,128)S(1)}) custom-call(s32[512]{0:T(512)S(1)} %reshape.56.asked, s32[128]{0:T(128)S(1)} %get-tuple-element.73.place, f32[16,3,128]{2,1,0:T(4,128)S(1)} %get-tuple-element.98.pos, ...), custom_call_target="tpu_custom_call" | custom-call | flops 10000000000 | tf_op jit(solution)/shard_map/density/pallas_call | solution.py:534
  284.1 10.5 %all_to_all.228 = f32[32,8,128]{2,1,0:T(8,128)S(1)} all-to-all(f32[32,8,128]{2,1,0:T(8,128)S(1)} %bitcast.72), channel_id=1, replica_groups=mesh['gx'=4,'gy'=8] {'gx','gy'}, dimensions={0} | all-to-all | bytes 262144 | tf_op jit(solution)/shard_map/density/all_to_all | solution.py:39
  294.6 2.0 force.6
  296.6 6.9 %all-to-all-start.13 = ((f32[32,24,128]{2,1,0:T(8,128)}), f32[32,24,128]{2,1,0:T(8,128)S(1)}, u32[]{:S(2)}, u32[]{:S(2)}) async-start(f32[32,24,128]{2,1,0:T(8,128)} %bitcast.25), calls=%async_computation.13 | async-start | bytes 786432 | tf_op jit(solution)/shard_map/force/all_to_all | solution.py:39
  303.6 1.2 copy-done.21
  304.8 4.9 %omega.12 = f32[256,128]{1,0:T(8,128)S(1)} custom-call(s32[592]{0:T(1024)S(1)} %get-tuple-element.80.list_c, s32[148]{0:T(256)S(1)} %get-tuple-element.81.list_slot, s32[1]{0:T(128)} %get-tuple-element.82.number, f32[16,3,128]{2,1,0:T(4,128)S(1)} %get-tuple-element.114.pos, f32[17,128,128]{2,1,0:T(8,128)S(1)} %copy-done.21, f32[256,8,128]{2,1,0:T(8,128)S(1)} %slice.8.star), custom_call_target="tpu_custom_call" | custom-call | flops 10000000000 | tf_op jit(solution)/shard_map/omega/pallas_call | solution.py:554
  309.7 7.3 %all-to-all-done.13 = f32[32,24,128]{2,1,0:T(8,128)S(1)} async-done(((f32[32,24,128]{2,1,0:T(8,128)}), f32[32,24,128]{2,1,0:T(8,128)S(1)}, u32[]{:S(2)}, u32[]{:S(2)}) %all-to-all-start.13) | async-done | bytes 393248 | tf_op jit(solution)/shard_map/force/all_to_all | solution.py:39
  317.0 11.4 %all_to_all.229 = f32[32,8,128]{2,1,0:T(8,128)S(1)} all-to-all(f32[32,8,128]{2,1,0:T(8,128)S(1)} %bitcast.76), channel_id=1, replica_groups=mesh['gx'=4,'gy'=8] {'gx','gy'}, dimensions={0} | all-to-all | bytes 262144 | tf_op jit(solution)/shard_map/omega/all_to_all | solution.py:39
  328.4 9.9 %all_to_all.230 = f32[32,8,128]{2,1,0:T(8,128)S(1)} all-to-all(f32[32,8,128]{2,1,0:T(8,128)S(1)} %bitcast.55), channel_id=1, replica_groups=mesh['gx'=4,'gy'=8] {'gx','gy'}, dimensions={0} | all-to-all | bytes 262144 | tf_op jit(solution)/shard_map/omega/all_to_all | solution.py:39
  338.3 1.2 copy-done.22
  339.6 8.9 %deposit.6 = (f32[16,128]{1,0:T(8,128)S(1)}, f32[16,3,128]{2,1,0:T(4,128)S(1)}, f32[16,128]{1,0:T(8,128)S(1)}, f32[16,16,128]{2,1,0:T(8,128)S(1)}, f32[1024,128]{1,0:T(8,128)S(1)}) custom-call(s32[512]{0:T(512)S(1)} %reshape.56.asked, s32[592]{0:T(1024)S(1)} %get-tuple-element.80.list_c, s32[148]{0:T(256)S(1)} %get-tuple-element.81.list_slot, ...), custom_call_target="tpu_custom_call" | custom-call | flops 10000000000 | tf_op jit(solution)/shard_map/deposit/pallas_call | solution.py:565
  348.5 26.3 %all_to_all.231 = f32[32,32,128]{2,1,0:T(8,128)S(1)} all-to-all(f32[32,32,128]{2,1,0:T(8,128)S(1)} %bitcast.46), channel_id=1, replica_groups=mesh['gx'=4,'gy'=8] {'gx','gy'}, dimensions={0} | all-to-all | bytes 1048576 | tf_op jit(solution)/shard_map/deposit/all_to_all | solution.py:39
  374.8 6.1 %density.7 = (f32[16,8,128]{2,1,0:T(8,128)S(1)}, f32[16,128]{1,0:T(8,128)S(1)}, f32[16,128]{1,0:T(8,128)S(1)}, f32[16,128]{1,0:T(8,128)S(1)}, f32[256,128]{1,0:T(8,128)S(1)}) custom-call(s32[512]{0:T(512)S(1)} %reshape.56.asked, s32[128]{0:T(128)S(1)} %get-tuple-element.73.place, f32[16,3,128]{2,1,0:T(4,128)S(1)} %get-tuple-element.114.pos, ...), custom_call_target="tpu_custom_call" | custom-call | flops 10000000000 | tf_op jit(solution)/shard_map/density/pallas_call | solution.py:534
  380.9 10.5 %all_to_all.232 = f32[32,8,128]{2,1,0:T(8,128)S(1)} all-to-all(f32[32,8,128]{2,1,0:T(8,128)S(1)} %bitcast.73), channel_id=1, replica_groups=mesh['gx'=4,'gy'=8] {'gx','gy'}, dimensions={0} | all-to-all | bytes 262144 | tf_op jit(solution)/shard_map/density/all_to_all | solution.py:39
  393.0 5.0 %omega.14 = f32[256,128]{1,0:T(8,128)S(1)} custom-call(s32[592]{0:T(1024)S(1)} %get-tuple-element.80.list_c, s32[148]{0:T(256)S(1)} %get-tuple-element.81.list_slot, s32[1]{0:T(128)} %get-tuple-element.82.number, f32[16,3,128]{2,1,0:T(4,128)S(1)} %get-tuple-element.149.pos, f32[17,128,128]{2,1,0:T(8,128)S(1)} %copy-done.23, f32[256,8,128]{2,1,0:T(8,128)S(1)} %copy-done.2), custom_call_target="tpu_custom_call" | custom-call | flops 10000000000 | tf_op jit(solution)/shard_map/omega/pallas_call | solution.py:554
  398.0 17.2 %all_to_all.233 = f32[32,8,128]{2,1,0:T(8,128)S(1)} all-to-all(f32[32,8,128]{2,1,0:T(8,128)S(1)} %bitcast.77), channel_id=1, replica_groups=mesh['gx'=4,'gy'=8] {'gx','gy'}, dimensions={0} | all-to-all | bytes 262144 | tf_op jit(solution)/shard_map/omega/all_to_all | solution.py:39
  415.9 2.4 all-to-all-start.19
  418.9 7.8 %all-to-all-done.19 = f32[32,8,128]{2,1,0:T(8,128)S(1)} async-done(((f32[32,8,128]{2,1,0:T(8,128)}), f32[32,8,128]{2,1,0:T(8,128)S(1)}, u32[]{:S(2)}, u32[]{:S(2)}) %all-to-all-start.19) | async-done | bytes 131104 | tf_op jit(solution)/shard_map/omega/all_to_all | solution.py:39
  426.6 1.2 copy-done.3
  427.8 1.2 copy-done.24
  429.1 7.6 %deposit.7 = (f32[16,128]{1,0:T(8,128)}, f32[16,3,128]{2,1,0:T(4,128)S(1)}, f32[16,128]{1,0:T(8,128)}, f32[16,16,128]{2,1,0:T(8,128)}) custom-call(s32[512]{0:T(512)S(1)} %reshape.56.asked, s32[592]{0:T(1024)S(1)} %get-tuple-element.80.list_c, s32[148]{0:T(256)S(1)} %get-tuple-element.81.list_slot, s32[1]{0:T(128)} %get-tuple-element.82.number, ...), custom_call_target="tpu_custom_call" | custom-call | flops 10000000000 | tf_op jit(solution)/shard_map/deposit/pallas_call | solution.py:565
  (62 shorter events, 12.6 us)
Async XLA Ops:
  7.2 101.4 %all-gather.2.cloned.1.call-start = ((), (), s32[]{:S(2)}) async-start(), calls=%async_computation.20 | async-start | bytes 4325376 | tf_op jit(solution)/shard_map/share/all_gather | solution.py:509
  8.6 0.8 copy-start.4
  9.5 0.7 copy-start.11
  10.2 0.7 copy-start.12
  10.8 0.7 copy-start.13
  13.8 0.7 copy-start.14
  14.5 0.7 copy-start.15
  19.0 13.8 %all-to-all-start = ((s32[32,1,16]{2,1,0:T(1,128)}), s32[32,1,16]{2,1,0:T(1,128)S(1)}, u32[]{:S(2)}, u32[]{:S(2)}) async-start(s32[32,1,16]{2,1,0:T(1,128)} %bitcast), calls=%async_computation | async-start | bytes 32768 | tf_op jit(solution)/shard_map/plan/all_to_all | solution.py:39
  34.1 0.7 copy-start.5
  34.8 0.7 copy-start.8
  37.8 48.9 %copy-start.16 = (f32[17,128,128]{2,1,0:T(8,128)}, f32[17,128,128]{2,1,0:T(8,128)S(1)}, u32[]{:S(2)}) copy-start(f32[17,128,128]{2,1,0:T(8,128)S(1)} %get-tuple-element.83.widths) | copy-start | bytes 3342340
  77.8 0.7 copy-start.6
  78.5 0.7 copy-start.9
  79.2 0.7 copy-start.26
  79.9 18.6 %copy-start.10 = (f32[16,128]{1,0:T(8,128)S(1)}, f32[16,128]{1,0:T(8,128)}, u32[]{:S(2)}) copy-start(f32[16,128]{1,0:T(8,128)} %smooth.17) | copy-start | bytes 24580
  79.9 18.6 %copy-start.27 = (f32[16,128]{1,0:T(8,128)S(1)}, f32[16,128]{1,0:T(8,128)}, u32[]{:S(2)}) copy-start(f32[16,128]{1,0:T(8,128)} %energy.3) | copy-start | bytes 24580
  79.9 18.6 %copy-start.28 = (s32[16]{0:T(128)S(1)}, s32[16]{0:T(128)}, u32[]{:S(2)}) copy-start(s32[16]{0:T(128)} %bins.7) | copy-start | bytes 196
  86.7 11.8 %all-to-all-start.2 = ((f32[32,8,128]{2,1,0:T(8,128)}), f32[32,8,128]{2,1,0:T(8,128)S(1)}, u32[]{:S(2)}, u32[]{:S(2)}) async-start(f32[32,8,128]{2,1,0:T(8,128)} %bitcast.3), calls=%async_computation.2 | async-start | bytes 262144 | tf_op jit(solution)/shard_map/density/all_to_all | solution.py:39
  105.7 16.3 %all-to-all-start.3 = ((f32[32,24,128]{2,1,0:T(8,128)}), f32[32,24,128]{2,1,0:T(8,128)S(1)}, u32[]{:S(2)}, u32[]{:S(2)}) async-start(f32[32,24,128]{2,1,0:T(8,128)} %bitcast.5), calls=%async_computation.3 | async-start | bytes 786432 | tf_op jit(solution)/shard_map/force/all_to_all | solution.py:39
  109.9 228.4 %copy-start.1 = (f32[256,8,128]{2,1,0:T(8,128)}, f32[256,8,128]{2,1,0:T(8,128)S(1)}, u32[]{:S(2)}) copy-start(f32[256,8,128]{2,1,0:T(8,128)S(1)} %slice.8.star) | copy-start | bytes 3145732
  109.9 1.6 copy-start.17
  135.8 10.8 %all-to-all-start.5 = ((f32[32,8,128]{2,1,0:T(8,128)}), f32[32,8,128]{2,1,0:T(8,128)S(1)}, u32[]{:S(2)}, u32[]{:S(2)}) async-start(f32[32,8,128]{2,1,0:T(8,128)} %bitcast.9), calls=%async_computation.5 | async-start | bytes 262144 | tf_op jit(solution)/shard_map/omega/all_to_all | solution.py:39
  138.2 8.4 %copy-start.7 = (f32[16,128]{1,0:T(8,128)S(1)}, f32[16,128]{1,0:T(8,128)}, u32[]{:S(2)}) copy-start(f32[16,128]{1,0:T(8,128)} %mass.5) | copy-start | bytes 24580
  138.2 8.4 %copy-start.25 = (f32[16,16,128]{2,1,0:T(8,128)S(1)}, f32[16,16,128]{2,1,0:T(8,128)}, u32[]{:S(2)}) copy-start(f32[16,16,128]{2,1,0:T(8,128)} %metals.1) | copy-start | bytes 393220
  146.6 1.2 copy-start.18
  201.7 18.5 %all-to-all-start.8 = ((f32[32,24,128]{2,1,0:T(8,128)}), f32[32,24,128]{2,1,0:T(8,128)S(1)}, u32[]{:S(2)}, u32[]{:S(2)}) async-start(f32[32,24,128]{2,1,0:T(8,128)} %bitcast.15), calls=%async_computation.8 | async-start | bytes 786432 | tf_op jit(solution)/shard_map/force/all_to_all | solution.py:39
  206.7 1.2 copy-start.19
  241.5 1.2 copy-start.20
  296.6 20.3 %all-to-all-start.13 = ((f32[32,24,128]{2,1,0:T(8,128)}), f32[32,24,128]{2,1,0:T(8,128)S(1)}, u32[]{:S(2)}, u32[]{:S(2)}) async-start(f32[32,24,128]{2,1,0:T(8,128)} %bitcast.25), calls=%async_computation.13 | async-start | bytes 786432 | tf_op jit(solution)/shard_map/force/all_to_all | solution.py:39
  303.6 1.2 copy-start.21
  338.3 1.2 copy-start.22
  391.4 1.2 copy-start.2
  391.4 1.6 copy-start.23
  393.0 33.6 %copy-start = (f32[256,24,128]{2,1,0:T(8,128)S(1)}, f32[256,24,128]{2,1,0:T(8,128)}, u32[]{:S(2)}) copy-start(f32[256,24,128]{2,1,0:T(8,128)} %slice.9.pay) | copy-start | bytes 9437188
  415.9 10.8 %all-to-all-start.19 = ((f32[32,8,128]{2,1,0:T(8,128)}), f32[32,8,128]{2,1,0:T(8,128)S(1)}, u32[]{:S(2)}, u32[]{:S(2)}) async-start(f32[32,8,128]{2,1,0:T(8,128)} %bitcast.37), calls=%async_computation.19 | async-start | bytes 262144 | tf_op jit(solution)/shard_map/omega/all_to_all | solution.py:39
  426.6 1.2 copy-start.3
  427.8 1.2 copy-start.24
Sparse Core Ops, SparseCore 0:
  12.4 73.0 all-gather.1

commit v3 on v2

--- a/solution.py
+++ b/solution.py
@@ -20,7 +20,7 @@
 TEAM = 4
 VMEM = pl.BlockSpec(memory_space=pltpu.VMEM)
 SMEM = pl.BlockSpec(memory_space=pltpu.SMEM)
-PARAMS = pltpu.CompilerParams(vmem_limit_bytes=48 * 1024 * 1024)
+PARAMS = pltpu.CompilerParams(vmem_limit_bytes=52 * 1024 * 1024)
 
 
 def call(body, outs, ins, scratch=(), smem_outs=(), work=0):
@@ -127,15 +127,14 @@
     return body
 
 
-def list_sizes(stars, nb):
-    room = stars + nb * GROUP + WIDE
-    room = -(-room // WIDE) * WIDE
+def list_sizes(hits, stars, nb):
+    room = -(-(hits + nb * (GROUP - 1)) // WIDE) * WIDE
     return room, room + stars
 
 
-def list_kernel(peers, cap, sb, nb):
+def list_kernel(peers, cap, sb, nb, hits):
     span = cap + sb
-    room, whole = list_sizes(peers * sb, nb)
+    room, whole = list_sizes(hits, peers * sb, nb)
 
     def body(asked, list_c, list_slot, number, count):
         for b in range(nb + 1):
@@ -178,28 +177,29 @@
     return body
 
 
-def send_rows(asked, out, source, width, cap, span):
+def send_rows(asked, out, source, cap, span):
+    width = source.shape[1]
+
     def one(d, _):
+        base = pl.multiple_of(d * (cap * width), cap * width)
         for c in range(cap):
             slot = jnp.maximum(asked[d * span + c], 0)
-            for f in range(width):
-                out[pl.ds((d * cap + c) * width + f, 1), :] = source(slot, f)
+            out[pl.ds(base + c * width, width), :] = source[slot]
         return 0
 
     lax.fori_loop(0, out.shape[0] // (cap * width), one, 0)
 
 
 def start_kernel(cap, span):
-    def body(asked, pos, vel, mass, smooth, send, widths):
-        def source(slot, f):
-            if f < 3:
-                return pos[slot, f : f + 1, :]
-            if f >= 5:
-                return vel[slot, f - 5 : f - 4, :]
-            return row_of(smooth if f == 3 else mass, slot)
-
-        send_rows(asked, send, source, 8, cap, span)
+    def body(asked, pos, vel, mass, smooth, send, widths, state):
         blocks = pos.shape[0]
+        for b in range(blocks):
+            h = smooth[b : b + 1, :]
+            state[b, 0:3, :] = pos[b]
+            state[b, 3:4, :] = h
+            state[b, 4:5, :] = mass[b : b + 1, :]
+            state[b, 5:8, :] = vel[b]
+        send_rows(asked, send, state, cap, span)
 
         def one(b, _):
             h = row_of(smooth, b)
@@ -256,9 +256,9 @@
 def density_kernel(neighbours, cap, span, first):
     def body(asked, place, pos, vel, mass, smooth, energy, *rest):
         if first:
-            far0, sums, term, gain, density, send_gain = rest
+            far0, sums, term, gain, density, send_gain, out_gain = rest
         else:
-            far_pos, far_mv, sums, term, gain, density, send_gain = rest
+            far_pos, far_mv, sums, term, gain, density, send_gain, out_gain = rest
 
         def ghost(at):
             if first:
@@ -290,13 +290,26 @@
                 density[pl.ds(b, 1), :] = dense
                 own = GAMMA_LESS * row_of(energy, b) / dense
                 term[pl.ds(b, 1), :] = own
-                gain[pl.ds(b, 1), :] = row_of(mass, b) * own * ((2.0 * KERNEL_NORM) / (h * h * h * h * h))
+                push = row_of(mass, b) * own * ((2.0 * KERNEL_NORM) / (h * h * h * h * h))
+                gain[pl.ds(b, 1), :] = push
+                out_gain[b] = push
             return 0
 
         lax.fori_loop(0, pos.shape[0] // TEAM, team, 0)
-        send_rows(asked, send_gain, lambda slot, f: row_of(gain, slot), 1, cap, span)
-
-    return body
+        send_rows(asked, send_gain, out_gain, cap, span)
+
+    return body
+
+
+def gas_sides(pos, sides):
+    def one(b, _):
+        x, y, z = (pos[b, f : f + 1, :] for f in range(3))
+        sides[b] = near_side(rows8(-2.0 * x, -2.0 * y, -2.0 * z, 1.0, norm_sq(x, y, z)))
+        return 0
+
+    blocks = pos.shape[0]
+    lax.fori_loop(0, blocks, one, 0, unroll=4)
+    sides[blocks] = jnp.zeros(sides.shape[1:], BF16)
 
 
 def force_kernel(neighbours, cap, span, substep, first, last):
@@ -361,21 +374,11 @@
             return 0
 
         lax.fori_loop(0, (used + TEAM - 1) // TEAM, team, 0)
+        gas_sides(new_pos, rest[-2])
         if not last:
-            send_rows(asked, rest[-2], lambda slot, f: new_pos[slot, f : f + 1, :], 3, cap, span)
-
-    return body
-
-
-def gas_sides(pos, sides):
-    def one(b, _):
-        x, y, z = (pos[b, f : f + 1, :] for f in range(3))
-        sides[b] = near_side(rows8(-2.0 * x, -2.0 * y, -2.0 * z, 1.0, norm_sq(x, y, z)))
-        return 0
-
-    blocks = pos.shape[0]
-    lax.fori_loop(0, blocks, one, 0, unroll=4)
-    sides[blocks] = jnp.zeros(sides.shape[1:], BF16)
+            send_rows(asked, rest[-3], new_pos, cap, span)
+
+    return body
 
 
 def omegas(list_c, list_slot, at, when, star, sides, widths):
@@ -399,8 +402,7 @@
 def omega_kernel(substep):
     when = (substep + 1) * TIME_STEP
 
-    def body(list_c, list_slot, number, pos, widths, star, part, sides, room):
-        gas_sides(pos, sides)
+    def body(list_c, list_slot, number, sides, widths, star, part, room):
         room[...] = jnp.zeros_like(room)
         trash = part.shape[0]
 
@@ -419,11 +421,10 @@
     when = (substep + 1) * TIME_STEP
 
     def body(
-        asked, list_c, list_slot, number, pos, widths, star, pay, total, mass, vel, energy, metals, density, *rest
+        asked, list_c, list_slot, number, sides, widths, star, pay, total, mass, vel, energy, metals, density, *rest
     ):
         new_mass, new_vel, new_energy, new_metals = rest[:4]
-        sides, dep = rest[-2:]
-        gas_sides(pos, sides)
+        dep = rest[-2]
         dep[...] = jnp.zeros_like(dep)
 
         def group(at, _):
@@ -454,7 +455,12 @@
             m = row_of(mass, b)
             grown = m + got[0:1]
             new_mass[pl.ds(b, 1), :] = grown
-            new_vel[b] = (m * vel[b] + got[1:4]) / grown
+            speed = (m * vel[b] + got[1:4]) / grown
+            new_vel[b] = speed
+            if not last:
+                state = rest[-1]
+                state[b, 0:1, :] = grown
+                state[b, 1:4, :] = speed
             cooled = ENERGY_FLOOR + (row_of(energy, b) - ENERGY_FLOOR) * jnp.exp(
                 (-TIME_STEP * COOL_RATE) * row_of(density, b)
             )
@@ -462,16 +468,9 @@
             new_metals[b] = metals[b] + got[8:24]
             return 0
 
-        lax.fori_loop(0, pos.shape[0], block, 0, unroll=4)
+        lax.fori_loop(0, mass.shape[0], block, 0, unroll=4)
         if not last:
-            send_rows(
-                asked,
-                rest[4],
-                lambda slot, f: new_vel[slot, f - 1 : f, :] if f else row_of(new_mass, slot),
-                4,
-                cap,
-                span,
-            )
+            send_rows(asked, rest[4], rest[-1], cap, span)
 
     return body
 
@@ -489,7 +488,8 @@
     stars = peers * sb
     sent = peers * cap
     i32 = jnp.int32
-    room, whole = list_sizes(stars, nb)
+    hits = peers * max(2, 2 * sb * star_ovl_dev.shape[1] // peers)
+    room, whole = list_sizes(hits, stars, nb)
     heavy = 10**10
 
     with jax.named_scope("plan"):
@@ -503,6 +503,7 @@
         asked = swap(req.reshape(peers, span)).reshape(-1)
 
     with jax.named_scope("share"):
+        req, star_pos, star_vel, star_yields = lax.optimization_barrier((req, star_pos, star_vel, star_yields))
         share = call(share_kernel, [((sb, 32, width), F32)], [VMEM] * 6)(
             star_pos, star_vel, star_radius, star_mdot, star_edot, star_yields
         )[0]
@@ -514,10 +515,11 @@
             start_kernel(cap, span),
             [((sent * 8, width), F32), ((nb + 1, width, width), F32)],
             [SMEM] + [VMEM] * 4,
+            [pltpu.VMEM((nb, 8, width), F32)],
         )(asked, gas_pos, gas_vel, gas_mass, gas_smooth)
         far0 = swap(send0)
         list_c, list_slot, number = call(
-            list_kernel(peers, cap, sb, nb),
+            list_kernel(peers, cap, sb, nb, hits),
             [((whole,), i32), ((whole // GROUP,), i32), ((1,), i32)],
             [SMEM],
             [pltpu.SMEM((nb + 1,), i32)],
@@ -525,7 +527,6 @@
         )(asked)
 
     pos, vel, mass, energy, metals = gas_pos, gas_vel, gas_mass, gas_energy, gas_metals
-    sides = pltpu.VMEM((nb + 1, width, 48), BF16)
     block3, block1 = ((nb, 3, width), F32), ((nb, width), F32)
     for substep in range(SUBSTEPS):
         first, last = substep == 0, substep == SUBSTEPS - 1
@@ -535,6 +536,7 @@
                 density_kernel(neighbours, cap, span, first),
                 [((nb, 8, width), F32), block1, block1, block1, ((sent, width), F32)],
                 [SMEM] * 2 + [VMEM] * (5 + len(far)),
+                [pltpu.VMEM((nb, 1, width), F32)],
                 work=heavy,
             )(asked, place, pos, vel, mass, gas_smooth, energy, *far)
             far_gain = swap(send_gain)
@@ -542,36 +544,37 @@
             far = [far0] if first else [far0, far_pos]
             outs = call(
                 force_kernel(neighbours, cap, span, substep, first, last),
-                [block3, block3, block1] + ([] if last else [((sent * 3, width), F32)]),
+                [block3, block3, block1] + ([] if last else [((sent * 3, width), F32)]) + [((nb + 1, width, 48), BF16)],
                 [SMEM] * 3 + [VMEM] * (8 + len(far)),
                 [pltpu.SMEM((nb + TEAM,), i32)],
                 work=heavy,
             )(asked, place, gas_bins, pos, vel, gas_smooth, energy, term, gain, sums, *far, far_gain)
             pos, vel, energy = outs[:3]
-            if not last:
-                far_pos = swap(outs[3])
+            sides = outs[-1]
         with jax.named_scope("omega"):
             part = call(
                 omega_kernel(substep),
                 [((stars, width), F32)],
                 [SMEM] * 3 + [VMEM] * 3,
-                [sides, pltpu.VMEM((stars + 8, width), F32)],
+                [pltpu.VMEM((stars + 8, width), F32)],
                 work=heavy,
-            )(list_c, list_slot, number, pos, widths, all_star8)[0]
+            )(list_c, list_slot, number, sides, widths, all_star8)[0]
+            total = swap(call(total_kernel(peers), [((stars, width), F32)], [VMEM])(swap(part))[0])
             if not last:
-                part, far_pos = lax.optimization_barrier((part, far_pos))
-            total = swap(call(total_kernel(peers), [((stars, width), F32)], [VMEM])(swap(part))[0])
+                total, send_pos = lax.optimization_barrier((total, outs[3]))
+                far_pos = swap(send_pos)
         with jax.named_scope("deposit"):
             outs = call(
                 deposit_kernel(substep, last, cap, span),
                 [block1, block3, block1, ((nb, 16, width), F32)] + ([] if last else [((sent * 4, width), F32)]),
                 [SMEM] * 4 + [VMEM] * 10,
-                [sides, pltpu.VMEM((nb + 1, width, 48), F32)],
+                [pltpu.VMEM((nb + 1, width, 48), F32), pltpu.VMEM((nb, 4, width), F32)],
                 work=heavy,
-            )(asked, list_c, list_slot, number, pos, widths, all_star8, all_pay, total, mass, vel, energy, metals, density)
+            )(asked, list_c, list_slot, number, sides, widths, all_star8, all_pay, total, mass, vel, energy, metals, density)
             mass, vel, energy, metals = outs[:4]
             if not last:
-                far_mv = swap(outs[4])
+                send_mv, far_pos = lax.optimization_barrier((outs[4], far_pos))
+                far_mv = swap(send_mv)
     return (pos, vel, mass, energy, metals)
 
 

time: 451 us -> 444 us (0.984)
  Pallas kernels: 104 us -> 180 us
  blocking collectives: 223 us -> 184 us
  waiting for transfers between devices: 40.8 us -> 20.7 us
  local copies, waits for them, and re-layouts: 31.1 us -> 19.8 us
  starting transfers between devices: 30.2 us -> 22.1 us
    all_to_all x13, blocking collectives: 223 us -> 184 us  [swap(): lax.all_to_all(payload, AXES, split_axis=0, concat_axis=0, tiled=True)]
    pallas_call x4, Pallas kernels: 34.4 us -> 71 us  [local(): call(deposit_kernel(substep, last, cap, span), [block1, block3, block1, (...]
    pallas_call x4, Pallas kernels: 19.6 us -> 43.3 us  [local(): call(omega_kernel(substep), [((stars, width), F32)], [SMEM] * 3 + [VMEM]...]
    all_to_all x7, waiting for transfers between devices: 40.8 us -> 20.7 us  [swap(): lax.all_to_all(payload, AXES, split_axis=0, concat_axis=0, tiled=True)]
    pallas_call x4, Pallas kernels: 11.8 us -> 26.6 us  [local(): call(force_kernel(neighbours, cap, span, substep, first, last), [block3,...]
    unnamed x66 -> x46, local copies, waits for them, and re-layouts: 24.7 us -> 12 us
    all_to_all x7, starting transfers between devices: 30.1 us -> 22 us  [swap(): lax.all_to_all(payload, AXES, split_axis=0, concat_axis=0, tiled=True)]
  transfers between devices with their start and end apart: 8 -> 8, of which waited for: 7 -> 4; matrix products, arithmetic and copies ran while one was open for 2% -> 2% of each run, Pallas kernels for 9% -> 17%
where the time goes in v3:
time: 444 us; the launch traced here: 441 us
  blocking collectives  184 us (41%)
  Pallas kernels  180 us (41%)
  starting transfers between devices  22.1 us (5%)
  waiting for transfers between devices  20.7 us (5%)
  local copies, waits for them, and re-layouts  19.8 us (4%)
  between operations  14.3 us (3%)
    all_to_all x13, blocking collectives, swap(): lax.all_to_all(payload, AXES, split_axis=0, concat_axis=0, tiled=True)  184 us
    pallas_call x4, Pallas kernels, local(): call(deposit_kernel(substep, last, cap, span), [block1, block3, block1, (...  71 us
    pallas_call x4, Pallas kernels, local(): call(omega_kernel(substep), [((stars, width), F32)], [SMEM] * 3 + [VMEM]...  43.3 us
    pallas_call x4, Pallas kernels, local(): call(force_kernel(neighbours, cap, span, substep, first, last), [block3,...  26.6 us
    pallas_call x4, Pallas kernels, local(): call(density_kernel(neighbours, cap, span, first), [((nb, 8, width), F32)...  25.2 us
    all_to_all x7, starting transfers between devices, swap(): lax.all_to_all(payload, AXES, split_axis=0, concat_axis=0, tiled=True)  22 us
    all_to_all x7, waiting for transfers between devices, swap(): lax.all_to_all(payload, AXES, split_axis=0, concat_axis=0, tiled=True)  20.7 us
    unnamed x46, local copies, waits for them, and re-layouts  12 us
  transfers between devices with their start and end apart: 8, of which 4 were waited for; matrix products, arithmetic and copies ran while one was open for 2% of the time, Pallas kernels for 17%

profile of v3, /device:TPU:1, one launch (start us, length us, event | category | flops | bytes accessed | tf_op | source)
XLA Modules:
  0.0 441.3 jit_solution(18260939028813885881)
XLA Ops:
  7.2 0.8 copy.46.gas_dev
  8.0 0.8 copy.47.gas_slot
  8.7 0.7 copy-done.15
  9.4 0.7 copy-done.16
  10.1 3.1 plan.1
  13.2 0.7 copy.55.star_pos
  13.9 0.7 copy.56.star_vel
  14.7 0.8 copy-done.5
  15.5 0.7 copy-done.12
  18.3 0.7 all_to_all.145
  18.9 7.1 %all-to-all-start = ((s32[32,1,16]{2,1,0:T(1,128)}), s32[32,1,16]{2,1,0:T(1,128)S(1)}, u32[]{:S(2)}, u32[]{:S(2)}) async-start(s32[32,1,16]{2,1,0:T(1,128)} %bitcast), calls=%async_computation | async-start | bytes 32768 | tf_op jit(solution)/shard_map/plan/all_to_all | solution.py:39
  26.0 0.8 copy.53.pos
  26.8 0.8 copy.54.vel
  27.6 5.2 %all-to-all-done = s32[32,1,16]{2,1,0:T(1,128)S(1)} async-done(((s32[32,1,16]{2,1,0:T(1,128)}), s32[32,1,16]{2,1,0:T(1,128)S(1)}, u32[]{:S(2)}, u32[]{:S(2)}) %all-to-all-start) | async-done | bytes 2080 | tf_op jit(solution)/shard_map/plan/all_to_all | solution.py:39
  33.3 0.7 reduce.3
  34.0 0.7 copy-done.6
  34.7 0.7 copy-done.9
  35.4 3.0 start.2
  38.5 34.9 %all_to_all.224 = f32[32,64,128]{2,1,0:T(8,128)S(1)} all-to-all(f32[32,64,128]{2,1,0:T(8,128)S(1)} %bitcast.44), channel_id=1, replica_groups=mesh['gx'=4,'gy'=8] {'gx','gy'}, dimensions={0} | all-to-all | bytes 2097152 | tf_op jit(solution)/shard_map/start/all_to_all | solution.py:39
  73.4 0.7 copy-done.7
  74.1 0.7 copy-done.10
  74.8 0.7 copy-done.18
  75.5 6.8 %density.4 = (f32[16,8,128]{2,1,0:T(8,128)S(1)}, f32[16,128]{1,0:T(8,128)S(1)}, f32[16,128]{1,0:T(8,128)S(1)}, f32[16,128]{1,0:T(8,128)S(1)}, f32[256,128]{1,0:T(8,128)}) custom-call(s32[512]{0:T(512)S(1)} %reshape.56.asked, s32[128]{0:T(128)S(1)} %get-tuple-element.86.place, f32[16,3,128]{2,1,0:T(4,128)S(1)} %copy.53.pos, f32[16,3,128]{2,1,0:T(4,128)S(1)} %copy.54.vel, ...), custom_call_target="tpu_custom_call" | custom-call | flops 10000000000 | tf_op jit(solution)/shard_map/density/pallas_call | solution.py:535
  82.3 3.0 all-to-all-start.2
  85.3 5.2 %start.3 = (s32[560]{0:T(1024)S(1)}, s32[140]{0:T(256)S(1)}, s32[1]{0:T(128)}) custom-call(s32[512]{0:T(512)S(1)} %reshape.56.asked), custom_call_target="tpu_custom_call" | custom-call | tf_op jit(solution)/shard_map/start/pallas_call | solution.py:521
  90.5 3.2 all-to-all-done.2
  93.7 8.1 %force.4 = (f32[16,3,128]{2,1,0:T(4,128)S(1)}, f32[16,3,128]{2,1,0:T(4,128)S(1)}, f32[16,128]{1,0:T(8,128)S(1)}, f32[768,128]{1,0:T(8,128)}, bf16[17,128,48]{2,1,0:T(8,128)(2,1)S(1)}) custom-call(s32[512]{0:T(512)S(1)} %reshape.56.asked, s32[128]{0:T(128)S(1)} %get-tuple-element.86.place, s32[16]{0:T(128)S(1)} %copy-done.19, f32[16,3,128]{2,1,0:T(4,128)S(1)} %copy.53.pos, ...), custom_call_target="tpu_custom_call" | custom-call | flops 10000000000 | tf_op jit(solution)/shard_map/force/pallas_call | solution.py:545
  101.8 1.3 slice.8.star
  103.1 10.9 %omega.8 = f32[256,128]{1,0:T(8,128)S(1)} custom-call(s32[560]{0:T(1024)S(1)} %get-tuple-element.93.list_c, s32[140]{0:T(256)S(1)} %get-tuple-element.94.list_slot, s32[1]{0:T(128)} %get-tuple-element.95.number, bf16[17,128,48]{2,1,0:T(8,128)(2,1)S(1)} %get-tuple-element.96.sides, f32[17,128,128]{2,1,0:T(8,128)} %get-tuple-element.97.widths, ...), custom_call_target="tpu_custom_call" | custom-call | flops 10000000000 | tf_op jit(solution)/shard_map/omega/pallas_call | solution.py:555
  114.0 9.5 %all_to_all.225 = f32[32,8,128]{2,1,0:T(8,128)S(1)} all-to-all(f32[32,8,128]{2,1,0:T(8,128)S(1)} %bitcast.74), channel_id=1, replica_groups=mesh['gx'=4,'gy'=8] {'gx','gy'}, dimensions={0} | all-to-all | bytes 262144 | tf_op jit(solution)/shard_map/omega/all_to_all | solution.py:39
  123.5 0.7 omega.9
  124.2 2.4 all-to-all-start.4
  126.6 3.8 slice.9.pay
  130.4 4.6 %all-to-all-done.4 = f32[32,8,128]{2,1,0:T(8,128)S(1)} async-done(((f32[32,8,128]{2,1,0:T(8,128)}), f32[32,8,128]{2,1,0:T(8,128)S(1)}, u32[]{:S(2)}, u32[]{:S(2)}) %all-to-all-start.4) | async-done | bytes 131104 | tf_op jit(solution)/shard_map/omega/all_to_all | solution.py:39
  135.0 2.4 all-to-all-start.5
  137.4 17.8 %deposit.4 = (f32[16,128]{1,0:T(8,128)S(1)}, f32[16,3,128]{2,1,0:T(4,128)S(1)}, f32[16,128]{1,0:T(8,128)S(1)}, f32[16,16,128]{2,1,0:T(8,128)S(1)}, f32[1024,128]{1,0:T(8,128)S(1)}) custom-call(s32[512]{0:T(512)S(1)} %reshape.56.asked, s32[560]{0:T(1024)S(1)} %get-tuple-element.93.list_c, s32[140]{0:T(256)S(1)} %get-tuple-element.94.list_slot, ...), custom_call_target="tpu_custom_call" | custom-call | flops 10000000000 | tf_op jit(solution)/shard_map/deposit/pallas_call | solution.py:567
  155.2 20.8 %all_to_all.226 = f32[32,32,128]{2,1,0:T(8,128)S(1)} all-to-all(f32[32,32,128]{2,1,0:T(8,128)S(1)} %bitcast.47), channel_id=1, replica_groups=mesh['gx'=4,'gy'=8] {'gx','gy'}, dimensions={0} | all-to-all | bytes 1048576 | tf_op jit(solution)/shard_map/deposit/all_to_all | solution.py:39
  176.1 6.1 %density.5 = (f32[16,8,128]{2,1,0:T(8,128)S(1)}, f32[16,128]{1,0:T(8,128)S(1)}, f32[16,128]{1,0:T(8,128)S(1)}, f32[16,128]{1,0:T(8,128)S(1)}, f32[256,128]{1,0:T(8,128)S(1)}) custom-call(s32[512]{0:T(512)S(1)} %reshape.56.asked, s32[128]{0:T(128)S(1)} %get-tuple-element.86.place, f32[16,3,128]{2,1,0:T(4,128)S(1)} %get-tuple-element.92.pos, ...), custom_call_target="tpu_custom_call" | custom-call | flops 10000000000 | tf_op jit(solution)/shard_map/density/pallas_call | solution.py:535
  182.2 10.5 %all_to_all.227 = f32[32,8,128]{2,1,0:T(8,128)S(1)} all-to-all(f32[32,8,128]{2,1,0:T(8,128)S(1)} %bitcast.71), channel_id=1, replica_groups=mesh['gx'=4,'gy'=8] {'gx','gy'}, dimensions={0} | all-to-all | bytes 262144 | tf_op jit(solution)/shard_map/density/all_to_all | solution.py:39
  192.7 5.7 %force.5 = (f32[16,3,128]{2,1,0:T(4,128)S(1)}, f32[16,3,128]{2,1,0:T(4,128)S(1)}, f32[16,128]{1,0:T(8,128)S(1)}, f32[768,128]{1,0:T(8,128)}, bf16[17,128,48]{2,1,0:T(8,128)(2,1)S(1)}) custom-call(s32[512]{0:T(512)S(1)} %reshape.56.asked, s32[128]{0:T(128)S(1)} %get-tuple-element.86.place, s32[16]{0:T(128)S(1)} %copy-done.19, ...), custom_call_target="tpu_custom_call" | custom-call | flops 10000000000 | tf_op jit(solution)/shard_map/force/pallas_call | solution.py:545
  198.4 10.8 %omega.10 = f32[256,128]{1,0:T(8,128)S(1)} custom-call(s32[560]{0:T(1024)S(1)} %get-tuple-element.93.list_c, s32[140]{0:T(256)S(1)} %get-tuple-element.94.list_slot, s32[1]{0:T(128)} %get-tuple-element.95.number, bf16[17,128,48]{2,1,0:T(8,128)(2,1)S(1)} %get-tuple-element.118.sides, f32[17,128,128]{2,1,0:T(8,128)} %get-tuple-element.97.widths, ...), custom_call_target="tpu_custom_call" | custom-call | flops 10000000000 | tf_op jit(solution)/shard_map/omega/pallas_call | solution.py:555
  209.3 8.7 %all_to_all.228 = f32[32,8,128]{2,1,0:T(8,128)S(1)} all-to-all(f32[32,8,128]{2,1,0:T(8,128)S(1)} %bitcast.75), channel_id=1, replica_groups=mesh['gx'=4,'gy'=8] {'gx','gy'}, dimensions={0} | all-to-all | bytes 262144 | tf_op jit(solution)/shard_map/omega/all_to_all | solution.py:39
  218.0 9.9 %all_to_all.229 = f32[32,8,128]{2,1,0:T(8,128)S(1)} all-to-all(f32[32,8,128]{2,1,0:T(8,128)S(1)} %bitcast.53), channel_id=1, replica_groups=mesh['gx'=4,'gy'=8] {'gx','gy'}, dimensions={0} | all-to-all | bytes 262144 | tf_op jit(solution)/shard_map/omega/all_to_all | solution.py:39
  227.9 2.4 all-to-all-start.10
  230.3 17.8 %deposit.5 = (f32[16,128]{1,0:T(8,128)S(1)}, f32[16,3,128]{2,1,0:T(4,128)S(1)}, f32[16,128]{1,0:T(8,128)S(1)}, f32[16,16,128]{2,1,0:T(8,128)S(1)}, f32[1024,128]{1,0:T(8,128)S(1)}) custom-call(s32[512]{0:T(512)S(1)} %reshape.56.asked, s32[560]{0:T(1024)S(1)} %get-tuple-element.93.list_c, s32[140]{0:T(256)S(1)} %get-tuple-element.94.list_slot, ...), custom_call_target="tpu_custom_call" | custom-call | flops 10000000000 | tf_op jit(solution)/shard_map/deposit/pallas_call | solution.py:567
  248.1 20.8 %all_to_all.230 = f32[32,32,128]{2,1,0:T(8,128)S(1)} all-to-all(f32[32,32,128]{2,1,0:T(8,128)S(1)} %bitcast.45), channel_id=1, replica_groups=mesh['gx'=4,'gy'=8] {'gx','gy'}, dimensions={0} | all-to-all | bytes 1048576 | tf_op jit(solution)/shard_map/deposit/all_to_all | solution.py:39
  268.9 6.1 %density.6 = (f32[16,8,128]{2,1,0:T(8,128)S(1)}, f32[16,128]{1,0:T(8,128)S(1)}, f32[16,128]{1,0:T(8,128)S(1)}, f32[16,128]{1,0:T(8,128)S(1)}, f32[256,128]{1,0:T(8,128)S(1)}) custom-call(s32[512]{0:T(512)S(1)} %reshape.56.asked, s32[128]{0:T(128)S(1)} %get-tuple-element.86.place, f32[16,3,128]{2,1,0:T(4,128)S(1)} %get-tuple-element.117.pos, ...), custom_call_target="tpu_custom_call" | custom-call | flops 10000000000 | tf_op jit(solution)/shard_map/density/pallas_call | solution.py:535
  275.1 10.5 %all_to_all.231 = f32[32,8,128]{2,1,0:T(8,128)S(1)} all-to-all(f32[32,8,128]{2,1,0:T(8,128)S(1)} %bitcast.72), channel_id=1, replica_groups=mesh['gx'=4,'gy'=8] {'gx','gy'}, dimensions={0} | all-to-all | bytes 262144 | tf_op jit(solution)/shard_map/density/all_to_all | solution.py:39
  285.6 8.3 %force.6 = (f32[16,3,128]{2,1,0:T(4,128)S(1)}, f32[16,3,128]{2,1,0:T(4,128)S(1)}, f32[16,128]{1,0:T(8,128)S(1)}, f32[768,128]{1,0:T(8,128)}, bf16[17,128,48]{2,1,0:T(8,128)(2,1)S(1)}) custom-call(s32[512]{0:T(512)S(1)} %reshape.56.asked, s32[128]{0:T(128)S(1)} %get-tuple-element.86.place, s32[16]{0:T(128)S(1)} %copy-done.19, ...), custom_call_target="tpu_custom_call" | custom-call | flops 10000000000 | tf_op jit(solution)/shard_map/force/pallas_call | solution.py:545
  293.9 10.8 %omega.12 = f32[256,128]{1,0:T(8,128)S(1)} custom-call(s32[560]{0:T(1024)S(1)} %get-tuple-element.93.list_c, s32[140]{0:T(256)S(1)} %get-tuple-element.94.list_slot, s32[1]{0:T(128)} %get-tuple-element.95.number, bf16[17,128,48]{2,1,0:T(8,128)(2,1)S(1)} %get-tuple-element.137.sides, f32[17,128,128]{2,1,0:T(8,128)} %get-tuple-element.97.widths, ...), custom_call_target="tpu_custom_call" | custom-call | flops 10000000000 | tf_op jit(solution)/shard_map/omega/pallas_call | solution.py:555
  304.7 8.7 %all_to_all.232 = f32[32,8,128]{2,1,0:T(8,128)S(1)} all-to-all(f32[32,8,128]{2,1,0:T(8,128)S(1)} %bitcast.76), channel_id=1, replica_groups=mesh['gx'=4,'gy'=8] {'gx','gy'}, dimensions={0} | all-to-all | bytes 262144 | tf_op jit(solution)/shard_map/omega/all_to_all | solution.py:39
  313.4 9.9 %all_to_all.233 = f32[32,8,128]{2,1,0:T(8,128)S(1)} all-to-all(f32[32,8,128]{2,1,0:T(8,128)S(1)} %bitcast.55), channel_id=1, replica_groups=mesh['gx'=4,'gy'=8] {'gx','gy'}, dimensions={0} | all-to-all | bytes 262144 | tf_op jit(solution)/shard_map/omega/all_to_all | solution.py:39
  323.3 2.4 all-to-all-start.15
  325.7 17.8 %deposit.6 = (f32[16,128]{1,0:T(8,128)S(1)}, f32[16,3,128]{2,1,0:T(4,128)S(1)}, f32[16,128]{1,0:T(8,128)S(1)}, f32[16,16,128]{2,1,0:T(8,128)S(1)}, f32[1024,128]{1,0:T(8,128)S(1)}) custom-call(s32[512]{0:T(512)S(1)} %reshape.56.asked, s32[560]{0:T(1024)S(1)} %get-tuple-element.93.list_c, s32[140]{0:T(256)S(1)} %get-tuple-element.94.list_slot, ...), custom_call_target="tpu_custom_call" | custom-call | flops 10000000000 | tf_op jit(solution)/shard_map/deposit/pallas_call | solution.py:567
  343.5 20.8 %all_to_all.234 = f32[32,32,128]{2,1,0:T(8,128)S(1)} all-to-all(f32[32,32,128]{2,1,0:T(8,128)S(1)} %bitcast.46), channel_id=1, replica_groups=mesh['gx'=4,'gy'=8] {'gx','gy'}, dimensions={0} | all-to-all | bytes 1048576 | tf_op jit(solution)/shard_map/deposit/all_to_all | solution.py:39
  364.3 6.1 %density.7 = (f32[16,8,128]{2,1,0:T(8,128)S(1)}, f32[16,128]{1,0:T(8,128)S(1)}, f32[16,128]{1,0:T(8,128)S(1)}, f32[16,128]{1,0:T(8,128)S(1)}, f32[256,128]{1,0:T(8,128)S(1)}) custom-call(s32[512]{0:T(512)S(1)} %reshape.56.asked, s32[128]{0:T(128)S(1)} %get-tuple-element.86.place, f32[16,3,128]{2,1,0:T(4,128)S(1)} %get-tuple-element.136.pos, ...), custom_call_target="tpu_custom_call" | custom-call | flops 10000000000 | tf_op jit(solution)/shard_map/density/pallas_call | solution.py:535
  370.5 10.5 %all_to_all.235 = f32[32,8,128]{2,1,0:T(8,128)S(1)} all-to-all(f32[32,8,128]{2,1,0:T(8,128)S(1)} %bitcast.73), channel_id=1, replica_groups=mesh['gx'=4,'gy'=8] {'gx','gy'}, dimensions={0} | all-to-all | bytes 262144 | tf_op jit(solution)/shard_map/density/all_to_all | solution.py:39
  381.0 4.4 force.7
  385.4 10.8 %omega.14 = f32[256,128]{1,0:T(8,128)S(1)} custom-call(s32[560]{0:T(1024)S(1)} %get-tuple-element.93.list_c, s32[140]{0:T(256)S(1)} %get-tuple-element.94.list_slot, s32[1]{0:T(128)} %get-tuple-element.95.number, bf16[17,128,48]{2,1,0:T(8,128)(2,1)S(1)} %get-tuple-element.156.sides, f32[17,128,128]{2,1,0:T(8,128)} %get-tuple-element.97.widths, ...), custom_call_target="tpu_custom_call" | custom-call | flops 10000000000 | tf_op jit(solution)/shard_map/omega/pallas_call | solution.py:555
  396.2 8.7 %all_to_all.236 = f32[32,8,128]{2,1,0:T(8,128)S(1)} all-to-all(f32[32,8,128]{2,1,0:T(8,128)S(1)} %bitcast.77), channel_id=1, replica_groups=mesh['gx'=4,'gy'=8] {'gx','gy'}, dimensions={0} | all-to-all | bytes 262144 | tf_op jit(solution)/shard_map/omega/all_to_all | solution.py:39
  404.9 0.7 omega.15
  405.6 2.4 all-to-all-start.19
  408.6 7.8 %all-to-all-done.19 = f32[32,8,128]{2,1,0:T(8,128)S(1)} async-done(((f32[32,8,128]{2,1,0:T(8,128)}), f32[32,8,128]{2,1,0:T(8,128)S(1)}, u32[]{:S(2)}, u32[]{:S(2)}) %all-to-all-start.19) | async-done | bytes 131104 | tf_op jit(solution)/shard_map/omega/all_to_all | solution.py:39
  416.3 17.5 %deposit.7 = (f32[16,128]{1,0:T(8,128)}, f32[16,3,128]{2,1,0:T(4,128)S(1)}, f32[16,128]{1,0:T(8,128)}, f32[16,16,128]{2,1,0:T(8,128)}) custom-call(s32[512]{0:T(512)S(1)} %reshape.56.asked, s32[560]{0:T(1024)S(1)} %get-tuple-element.93.list_c, s32[140]{0:T(256)S(1)} %get-tuple-element.94.list_slot, s32[1]{0:T(128)} %get-tuple-element.95.number, ...), custom_call_target="tpu_custom_call" | custom-call | flops 10000000000 | tf_op jit(solution)/shard_map/deposit/pallas_call | solution.py:567
  (44 shorter events, 4.1 us)
Async XLA Ops:
  7.2 94.6 %all-gather.2.cloned.1.call-start = ((), (), s32[]{:S(2)}) async-start(), calls=%async_computation.20 | async-start | bytes 4325376 | tf_op jit(solution)/shard_map/share/all_gather | solution.py:510
  8.7 0.7 copy-start.15
  9.4 0.7 copy-start.16
  14.6 0.8 copy-start.5
  15.5 0.7 copy-start.12
  16.2 0.7 copy-start.13
  16.9 0.7 copy-start.14
  18.9 13.8 %all-to-all-start = ((s32[32,1,16]{2,1,0:T(1,128)}), s32[32,1,16]{2,1,0:T(1,128)S(1)}, u32[]{:S(2)}, u32[]{:S(2)}) async-start(s32[32,1,16]{2,1,0:T(1,128)} %bitcast), calls=%async_computation | async-start | bytes 32768 | tf_op jit(solution)/shard_map/plan/all_to_all | solution.py:39
  34.0 0.7 copy-start.6
  34.7 0.7 copy-start.9
  73.4 8.9 %copy-start = (f32[32,64,128]{2,1,0:T(8,128)}, f32[32,64,128]{2,1,0:T(8,128)S(1)}, u32[]{:S(2)}) copy-start(f32[32,64,128]{2,1,0:T(8,128)S(1)} %all_to_all.224) | copy-start | bytes 3145732
  73.4 0.7 copy-start.7
  74.1 0.7 copy-start.10
  74.8 0.7 copy-start.18
  75.5 18.2 %copy-start.11 = (f32[16,128]{1,0:T(8,128)S(1)}, f32[16,128]{1,0:T(8,128)}, u32[]{:S(2)}) copy-start(f32[16,128]{1,0:T(8,128)} %smooth.17) | copy-start | bytes 24580
  75.5 18.2 %copy-start.19 = (s32[16]{0:T(128)S(1)}, s32[16]{0:T(128)}, u32[]{:S(2)}) copy-start(s32[16]{0:T(128)} %bins.7) | copy-start | bytes 196
  82.3 11.4 %all-to-all-start.2 = ((f32[32,8,128]{2,1,0:T(8,128)}), f32[32,8,128]{2,1,0:T(8,128)S(1)}, u32[]{:S(2)}, u32[]{:S(2)}) async-start(f32[32,8,128]{2,1,0:T(8,128)} %bitcast.3), calls=%async_computation.2 | async-start | bytes 262144 | tf_op jit(solution)/shard_map/density/all_to_all | solution.py:39
  103.1 10.9 %copy-start.1 = (f32[256,8,128]{2,1,0:T(8,128)}, f32[256,8,128]{2,1,0:T(8,128)S(1)}, u32[]{:S(2)}) copy-start(f32[256,8,128]{2,1,0:T(8,128)S(1)} %slice.8.star) | copy-start | bytes 3145732
  124.2 10.8 %all-to-all-start.4 = ((f32[32,8,128]{2,1,0:T(8,128)}), f32[32,8,128]{2,1,0:T(8,128)S(1)}, u32[]{:S(2)}, u32[]{:S(2)}) async-start(f32[32,8,128]{2,1,0:T(8,128)} %bitcast.7), calls=%async_computation.4 | async-start | bytes 262144 | tf_op jit(solution)/shard_map/omega/all_to_all | solution.py:39
  126.6 10.8 %copy-start.8 = (f32[16,128]{1,0:T(8,128)S(1)}, f32[16,128]{1,0:T(8,128)}, u32[]{:S(2)}) copy-start(f32[16,128]{1,0:T(8,128)} %mass.5) | copy-start | bytes 24580
  126.6 10.8 %copy-start.17 = (f32[16,16,128]{2,1,0:T(8,128)S(1)}, f32[16,16,128]{2,1,0:T(8,128)}, u32[]{:S(2)}) copy-start(f32[16,16,128]{2,1,0:T(8,128)} %metals.1) | copy-start | bytes 393220
  135.0 20.2 %all-to-all-start.5 = ((f32[32,24,128]{2,1,0:T(8,128)}), f32[32,24,128]{2,1,0:T(8,128)S(1)}, u32[]{:S(2)}, u32[]{:S(2)}) async-start(f32[32,24,128]{2,1,0:T(8,128)} %bitcast.9), calls=%async_computation.5 | async-start | bytes 786432 | tf_op jit(solution)/shard_map/omega/all_to_all | solution.py:39
  192.7 5.7 %copy-start.2 = (f32[256,8,128]{2,1,0:T(8,128)S(1)}, f32[256,8,128]{2,1,0:T(8,128)}, u32[]{:S(2)}) copy-start(f32[256,8,128]{2,1,0:T(8,128)} %copy-done.1) | copy-start | bytes 3145732
  227.9 20.2 %all-to-all-start.10 = ((f32[32,24,128]{2,1,0:T(8,128)}), f32[32,24,128]{2,1,0:T(8,128)S(1)}, u32[]{:S(2)}, u32[]{:S(2)}) async-start(f32[32,24,128]{2,1,0:T(8,128)} %bitcast.19), calls=%async_computation.10 | async-start | bytes 786432 | tf_op jit(solution)/shard_map/omega/all_to_all | solution.py:39
  285.6 8.3 %copy-start.3 = (f32[256,8,128]{2,1,0:T(8,128)S(1)}, f32[256,8,128]{2,1,0:T(8,128)}, u32[]{:S(2)}) copy-start(f32[256,8,128]{2,1,0:T(8,128)} %copy-done.1) | copy-start | bytes 3145732
  323.3 20.3 %all-to-all-start.15 = ((f32[32,24,128]{2,1,0:T(8,128)}), f32[32,24,128]{2,1,0:T(8,128)S(1)}, u32[]{:S(2)}, u32[]{:S(2)}) async-start(f32[32,24,128]{2,1,0:T(8,128)} %bitcast.29), calls=%async_computation.15 | async-start | bytes 786432 | tf_op jit(solution)/shard_map/omega/all_to_all | solution.py:39
  381.0 4.4 %copy-start.4 = (f32[256,8,128]{2,1,0:T(8,128)S(1)}, f32[256,8,128]{2,1,0:T(8,128)}, u32[]{:S(2)}) copy-start(f32[256,8,128]{2,1,0:T(8,128)} %copy-done.1) | copy-start | bytes 3145732
  405.6 10.8 %all-to-all-start.19 = ((f32[32,8,128]{2,1,0:T(8,128)}), f32[32,8,128]{2,1,0:T(8,128)S(1)}, u32[]{:S(2)}, u32[]{:S(2)}) async-start(f32[32,8,128]{2,1,0:T(8,128)} %bitcast.37), calls=%async_computation.19 | async-start | bytes 262144 | tf_op jit(solution)/shard_map/omega/all_to_all | solution.py:39
Sparse Core Ops, SparseCore 0:
  18.4 69.6 all-gather.1
